TPU v7x, 512 devices: a whole 4x8x8 slice. The times are simulated.
512 devices in a mesh: ctx: 64 (over y_lo, z, core), head: 8 (over y_hi, x).
Axes of the slice: x: 4, y: 8 (y_hi: 2, y_lo: 4; y = y_hi * 4 + y_lo), z: 8, core: 2. Of those that a mesh axis runs over, the one named last changes fastest.
Arguments:
- span_query: bfloat16 [4096, 12288], P('ctx', 'head'), may hold values from -106 to 106
- span_latent: bfloat16 [4096, 576], P('ctx'), may hold values from -12.5 to 12.5
- cache_latent: bfloat16 [1024, 576], P('ctx'), may hold values from -6 to 6
- cache_length: int32 [1], replicated, may hold values from 512 to 1024
- kv_up_weight: bfloat16 [512, 16384], P(None, 'head'), may hold values from -0.25 to 0.25
- out_weight: bfloat16 [8192, 7168], P('head', 'ctx'), may hold values from -0.5 to 0.5
Outputs:
- mixed: bfloat16 [4096, 7168], P('head', 'ctx')
All inputs are finite; a program needn't handle non-finite values.
Results may differ from a plain program's by a relative error of at most 0.019.
Values may be sent and summed in bfloat16 or wider, within the bound.
A program may use at most 64 MiB of HBM per device.

v0:
```python
import math

import jax
import jax.numpy as jnp
from jax import lax
from jax.sharding import PartitionSpec as P

LATENT = 512
ROPE = 64
NOPE = 128
VDIM = 128


mscale_factor = (1.0 + 0.1 * math.log(40.0)) ** 2
masked_score = -1e30


def update(running, part_queries, block_keys, allowed, score_scale):
    maxima, totals, accumulated = running
    scores = (
        jnp.einsum("qhc,rc->qhr", part_queries, block_keys, preferred_element_type=jnp.float32)
        * score_scale
    )
    scores = jnp.where(allowed[:, None, :], scores, masked_score)
    raised = jnp.maximum(maxima, jnp.max(scores, axis=2))
    weights = jnp.where(allowed[:, None, :], jnp.exp(scores - raised[:, :, None]), 0.0)
    factor = jnp.exp(maxima - raised)
    totals = totals * factor + jnp.sum(weights, axis=2)
    accumulated = accumulated * factor[:, :, None] + jnp.einsum(
        "qhr,rc->qhc",
        weights.astype(jnp.bfloat16),
        block_keys[:, :LATENT],
        preferred_element_type=jnp.float32,
    )
    return (raised, totals, accumulated)


def masked_update(member, part_queries, part_tokens, block_keys, key_index, score_scale):
    allowed = key_index[None, :] <= part_tokens[:, None]

    def attend_block(current):
        return update(current, part_queries, block_keys, allowed, score_scale)

    def keep_state(current):
        return current

    return lax.cond(key_index[0] <= jnp.max(part_tokens), attend_block, keep_state, member)


def on_device(span_query, span_latent, cache_latent, cache_length, kv_up_weight, out_weight):
    ctx_place = lax.axis_index("ctx")
    tok_rows = span_query.shape[0]
    score_scale = mscale_factor / math.sqrt(NOPE + ROPE)
    local_heads = kv_up_weight.shape[1] // (NOPE + VDIM)
    kv_shaped = kv_up_weight.reshape(LATENT, local_heads, NOPE + VDIM)
    own_index = ctx_place * tok_rows + jnp.arange(tok_rows, dtype=jnp.int32)
    bounds = ((0, tok_rows),)
    shaped = span_query.reshape(tok_rows, local_heads, NOPE + ROPE)
    absorbed = jnp.einsum(
        "thn,chn->thc",
        shaped[:, :, :NOPE],
        kv_shaped[:, :, :NOPE],
        preferred_element_type=jnp.float32,
    ).astype(jnp.bfloat16)
    queries = jnp.concatenate([absorbed, shaped[:, :, NOPE:]], axis=2)
    valid_cache = cache_length[0]
    start_state = (
        jnp.full((tok_rows, local_heads), masked_score, jnp.float32),
        jnp.zeros((tok_rows, local_heads), jnp.float32),
        jnp.zeros((tok_rows, local_heads, LATENT), jnp.float32),
    )
    piece = lax.all_gather(cache_latent, "ctx", axis=0, tiled=True)
    key_index = jnp.arange(piece.shape[0], dtype=jnp.int32)
    allowed = jnp.broadcast_to(key_index[None, :] < valid_cache, (tok_rows, piece.shape[0]))
    cache_state = update(start_state, queries, piece, allowed, score_scale)
    members = tuple(
        (tuple((member_part for member_part in cache_state)) for first_row, last_row in bounds)
    )
    piece = lax.all_gather(span_latent, "ctx", axis=0, tiled=True)
    piece_rows = piece.shape[0]
    block_goal = tok_rows * max(1, 512 // tok_rows)
    stacked = piece.reshape(piece_rows // block_goal, block_goal, piece.shape[1])
    offsets = block_goal * jnp.arange(piece_rows // block_goal, dtype=jnp.int32)

    def one_block(inner_states, scanned):
        block_keys, block_start = scanned
        key_index = block_start + jnp.arange(block_goal, dtype=jnp.int32)
        updated = []
        for (first_row, last_row), member in zip(bounds, inner_states):
            updated.append(
                masked_update(member, queries, own_index, block_keys, key_index, score_scale)
            )
        return (tuple(updated), None)

    result, unused = lax.scan(one_block, members, (stacked, offsets))
    members = result
    outputs = []
    for member in members:
        maxima, totals, accumulated = member
        latent_out = (accumulated / totals[:, :, None]).astype(jnp.bfloat16)
        outputs.append(
            jnp.einsum(
                "qhc,chv->qhv",
                latent_out,
                kv_shaped[:, :, NOPE:],
                preferred_element_type=jnp.float32,
            ).astype(jnp.bfloat16)
        )
    attended = outputs[0].reshape(tok_rows, local_heads * VDIM)
    terms = jnp.dot(
        lax.all_gather(attended, "ctx", axis=0, tiled=True),
        out_weight,
        preferred_element_type=jnp.float32,
    )
    return lax.psum_scatter(terms.astype(jnp.bfloat16), "head", scatter_dimension=0, tiled=True)


def solution(mesh):
    return jax.shard_map(
        on_device,
        mesh=mesh,
        in_specs=(
            P("ctx", "head"),
            P("ctx", None),
            P("ctx", None),
            P(),
            P(None, "head"),
            P("head", "ctx"),
        ),
        out_specs=P("head", "ctx"),
        check_vma=False,
    )
```

profile of v0, /device:TPU:2, one launch (start us, length us, event | category | flops | bytes accessed | tf_op | source)
XLA Modules:
  0.0 549.4 jit_solution(7541848966013170499)
XLA Ops:
  6.5 0.7 all-gather.4.cloned.1.call-update
  7.3 0.7 all-gather.6.cloned.1.call-update
  8.1 1.2 reshape.34
  9.3 0.7 add_reduce_fusion
  10.7 2.9 copy.34
  13.6 0.3 fusion.15
  14.0 116.8 %all-gather.4.cloned.1.call-done = bf16[1024,576]{1,0:T(8,128)(2,1)} async-done(((bf16[16,576]{1,0:T(8,128)(2,1)}), bf16[1024,576]{1,0:T(8,128)(2,1)}) %all-gather.4.cloned.1.call-update) | async-done | bytes 1179664 | tf_op jit(solution)/shard_map/all_gather | solution.py:72
  130.7 3.8 fusion.10
  134.6 2.4 fusion.12
  137.0 2.1 convolution_add_fusion.1
  139.1 113.4 %all-gather.6.cloned.1.call-done = bf16[4096,576]{1,0:T(8,128)(2,1)} async-done(((bf16[64,576]{1,0:T(8,128)(2,1)}), bf16[4096,576]{1,0:T(8,128)(2,1)}) %all-gather.6.cloned.1.call-update) | async-done | bytes 4718608 | tf_op jit(solution)/shard_map/all_gather | solution.py:79
  252.5 7.7 %copy.42 = bf16[8,512,576]{1,2,0:T(8,128)(2,1)} copy(bf16[8,512,576]{2,1,0:T(8,128)(2,1)} %bitcast.44) | data formatting | bytes 9437184
  260.2 31.3 %while.16 = (s32[]{:T(128)}, f32[64,8]{0,1:T(8,128)S(1)}, f32[64,8]{0,1:T(8,128)S(1)}, f32[64,8,512]{2,1,0:T(8,128)S(1)}, s32[8]{0:T(128)S(1)}, /*index=5*/s32[]...) while((s32[]{:T(128)}, f32[64,8]{0,1:T(8,128)S(1)}, ...), condition=%wide.region_8.9_spmd.clone, body=%wide.region_3.8_spmd.clone.sunk | while | flops 572819520 | bytes 8302375 | solution.py:95
  260.2 0.6 dynamic_slice.21
  260.8 0.6 iota_add_fusion.2
  261.5 0.6 slice.44
  263.5 4.7 conditional.3
  263.5 0.6 broadcast_add_fusion
  264.2 1.7 fusion.32
  266.0 1.1 dynamic-slice_bitcast_fusion
  267.1 0.4 fusion.4
  267.6 0.6 convolution_add_fusion
  268.2 0.7 dynamic_slice.21
  268.9 0.6 iota_add_fusion.2
  269.5 0.6 slice.44
  271.5 0.7 dynamic_slice.21
  272.2 0.6 iota_add_fusion.2
  272.8 0.6 slice.44
  274.9 0.7 dynamic_slice.21
  275.5 0.6 iota_add_fusion.2
  276.2 0.6 slice.44
  278.2 0.7 dynamic_slice.21
  278.8 0.6 iota_add_fusion.2
  279.5 0.6 slice.44
  281.5 0.7 dynamic_slice.21
  282.2 0.6 iota_add_fusion.2
  282.8 0.6 slice.44
  284.9 0.7 dynamic_slice.21
  285.5 0.6 iota_add_fusion.2
  286.1 0.6 slice.44
  288.2 0.7 dynamic_slice.21
  288.8 0.6 iota_add_fusion.2
  289.5 0.6 slice.44
  291.7 1.7 fusion.16
  293.4 0.7 copy.67
  294.2 152.4 %all-gather.8.cloned.1.call-done = bf16[4096,1024]{1,0:T(8,128)(2,1)} async-done(((bf16[64,1024]{1,0:T(8,128)(2,1)}), bf16[4096,1024]{1,0:T(8,128)(2,1)}) %all-gather.8.cloned.1.call-update) | async-done | bytes 8388624 | tf_op jit(solution)/shard_map/all_gather | solution.py:111
  446.6 7.2 %convolution_convert_fusion = bf16[4096,112]{0,1:T(8,128)(2,1)} fusion(bf16[4096,1024]{1,0:T(8,128)(2,1)} %all-gather.8.cloned.1.call-done, bf16[1024,112]{0,1:T(8,128)(2,1)S(1)} %copy-done), kind=kOutput, calls=%fused_computation.20 | convolution fusion | flops 939982848 | bytes 9535488 | tf_op jit(solution)/shard_map/dot_general | solution.py:110
  453.8 89.1 %reduce-scatter.2.cloned.1.call-done = bf16[512,112]{0,1:T(8,128)(2,1)} async-done(((bf16[4096,112]{0,1:T(8,128)(2,1)}), bf16[512,112]{0,1:T(8,128)(2,1)}) %reduce-scatter.2.cloned.1.call-update) | async-done | bytes 114704 | tf_op jit(solution)/shard_map/reduce_scatter | solution.py:115
  (57 shorter events, 1.0 us)
Async XLA Ops:
  6.5 440.1 %copy-start = (bf16[1024,112]{0,1:T(8,128)(2,1)S(1)}, bf16[1024,112]{0,1:T(8,128)(2,1)}, u32[]{:S(2)}) copy-start(bf16[1024,112]{0,1:T(8,128)(2,1)} %param.15) | copy-start | bytes 688132
  6.5 124.2 %all-gather.4.cloned.1.call-start = ((), (), s32[]{:S(2)}) async-start(), calls=%async_computation.1 | async-start | bytes 1331200 | tf_op jit(solution)/shard_map/all_gather | solution.py:72
  7.3 245.2 %all-gather.6.cloned.1.call-start = ((), (), s32[]{:S(2)}) async-start(), calls=%async_computation.2 | async-start | bytes 5324800 | tf_op jit(solution)/shard_map/all_gather | solution.py:79
  8.0 438.6 %all-gather.8.cloned.1.call-start = ((), (), s32[]{:S(2)}) async-start(), calls=%async_computation.3 | async-start | bytes 8519680 | tf_op jit(solution)/shard_map/all_gather | solution.py:111
  13.5 120.9 %copy-start.1 = (bf16[512,2048]{0,1:T(8,128)(2,1)}, bf16[512,2048]{0,1:T(8,128)(2,1)S(1)}, u32[]{:S(2)}) copy-start(bf16[512,2048]{0,1:T(8,128)(2,1)S(1)} %copy.34) | copy-start | bytes 6291460
  14.0 120.5 %copy-start.3 = (bf16[64,8,576]{2,0,1:T(8,128)(2,1)}, bf16[64,8,576]{2,0,1:T(8,128)(2,1)S(1)}, u32[]{:S(2)}) copy-start(bf16[64,8,576]{2,0,1:T(8,128)(2,1)S(1)} %pad_maximum_fusion) | copy-start | bytes 1769476
  134.5 2.5 copy-start.2
  252.5 7.7 %copy-start.4 = (bf16[64,8,576]{2,0,1:T(8,128)(2,1)S(1)}, bf16[64,8,576]{2,0,1:T(8,128)(2,1)}, u32[]{:S(2)}) copy-start(bf16[64,8,576]{2,0,1:T(8,128)(2,1)} %copy-done.3) | copy-start | bytes 1769476
  294.2 248.7 %reduce-scatter.2.cloned.1.call-start = ((), (), s32[]{:S(2)}) async-start(), calls=%async_computation.4 | async-start | bytes 1032192 | tf_op jit(solution)/shard_map/reduce_scatter | solution.py:115
Sparse Core Ops, SparseCore 0:
  9.5 121.1 all-gather.3
  132.9 119.5 all-gather.5
  294.3 152.2 all-gather.7
  454.0 88.9 reduce-scatter.1
where the time goes:
time: 551 us; the launch traced here: 549 us
  waiting for transfers between devices  473 us (86%)
  local copies, waits for them, and re-layouts  23.9 us (4%)
  matrix products  17.3 us (3%)
  between operations  13.9 us (3%)
  loops' own time  11.6 us (2%)
  other arithmetic  9.47 us (2%)
    all_gather x1, waiting for transfers between devices, on_device(): lax.all_gather(attended, 'ctx', axis=0, tiled=True)  152 us
    all_gather x1, waiting for transfers between devices, on_device(): piece = lax.all_gather(cache_latent, 'ctx', axis=0, tiled=True)  117 us
    all_gather x1, waiting for transfers between devices, on_device(): piece = lax.all_gather(span_latent, 'ctx', axis=0, tiled=True)  113 us
    reduce_scatter x1, waiting for transfers between devices, on_device(): lax.psum_scatter(terms.astype(jnp.bfloat16), 'head', scatter_dimension=0,...  89.1 us
    another operation x1, loops' own time, on_device(): result, unused = lax.scan(one_block, members, (stacked, offsets))  11.4 us
  transfers between devices with their start and end apart: 4, of which 4 were waited for; matrix products, arithmetic and copies ran while one was open for 2% of the time, Pallas kernels for 0%

commit v1 on v0

v1 whole, which is shorter than its diff:
```python
import math

import jax
import jax.numpy as jnp
from jax import lax
from jax.experimental import pallas as pl
from jax.experimental.pallas import tpu as pltpu
from jax.sharding import PartitionSpec as P

LATENT = 512
ROPE = 64
NOPE = 128
VDIM = 128
HEADS = 8
TOK = 64
CROWS = 16
SHARD = TOK + CROWS
WIDE = 640
HALF = 4 * SHARD
BLOCK = 2 * HALF
COLS = 112
ROWS = HEADS * TOK
CHUNK = 256
MASKED = -1e30
FAR = 1 << 30
MESH = pl.DeviceIdType.MESH
SCALE2 = (1.0 + 0.1 * math.log(40.0)) ** 2 / math.sqrt(NOPE + ROPE) * math.log2(math.e)


def kernel(
    query_ref,
    span_ref,
    cache_ref,
    length_ref,
    kv_ref,
    w_ref,
    out_ref,
    keys,
    mine,
    queries,
    maxima,
    totals,
    acc,
    latent_out,
    wbuf,
    att,
    part,
    landed,
    reduced,
    final,
    s_pre,
    s_ring,
    s_leaf,
    s_sib,
    s_w,
    s_wsib,
    s_att,
    s_x,
    s_f,
    r_ring,
    r_leaf,
    r_sib,
    r_w,
    r_att,
    r_x,
    r_f,
):
    ctx = lax.axis_index("ctx")
    head = lax.axis_index("head")
    x, yh = head % 4, head // 4
    q, z, c = ctx // 16, (ctx // 2) % 8, ctx % 2
    y = yh * 4 + q

    def device(dx, dy, dz, dc):
        return {"ctx": ((dy % 4) * 8 + dz) * 2 + dc, "head": (dy // 4) * 4 + dx}

    z_up = device(x, y, (z + 1) % 8, c)
    z_down = device(x, y, (z + 7) % 8, c)
    sibling = device(x, y, z, 1 - c)
    lead = jnp.where(c == 0, x, q)
    two = jnp.where(q % 2 == 0, 2, 6)

    def leaf(delta):
        step = two if delta == 2 else (delta if delta == 1 else 7)
        return device(
            jnp.where(c == 0, (x + delta) % 4, x), jnp.where(c == 0, y, (y + step) % 8), z, c
        )

    x0 = 2 * (q % 2)
    role = (x - x0 + 4) % 4
    my_j = jnp.where((role == 1) | (role == 2), 1, 0)
    my_pair = role // 2

    def target(b):
        return x0 + my_j, 4 * (q // 2) + 2 * my_pair + b // 2, b % 2

    def is_me(dx, dy, dc):
        return (dx == x) & (dy == y) & (dc == c)

    def copy(src, dst, ssem, rsem, dev):
        return pltpu.make_async_remote_copy(
            src_ref=src, dst_ref=dst, send_sem=ssem, recv_sem=rsem, device_id=dev, device_id_type=MESH
        )

    barrier = pltpu.get_barrier_semaphore()

    def greet(dev):
        pl.semaphore_signal(barrier, inc=1, device_id=dev, device_id_type=MESH)

    greet(z_up)
    greet(z_down)
    greet(sibling)
    for d in (1, 2, 3):
        greet(device((x + d) % 4, y, z, c))
        greet(device(x, yh * 4 + (q + d) % 4, z, c))
    for d in (1, 2, 6, 7):
        greet(device(x, (y + d) % 8, z, c))
    src_q = 2 * yh + x // 2
    src_j = x % 2
    src_x = jnp.where(q // 2 == 0, x, (2 * (x // 2) + 3 - src_j) % 4)
    for b in range(4):
        sx, sy, sc = src_x, src_q + 4 * (b // 2), b % 2

        @pl.when(jnp.logical_not(is_me(sx, sy, sc)))
        def _():
            greet(device(sx, sy, z, sc))

    selfs = 0
    for b in range(4):
        selfs = selfs + jnp.where(is_me(*target(b)), 1, 0)

    mine[:CROWS, :LATENT] = cache_ref[:, :LATENT]
    mine[CROWS:, :LATENT] = span_ref[:, :LATENT]
    mine[:CROWS, LATENT:] = jnp.concatenate(
        [cache_ref[:, LATENT:], jnp.zeros((CROWS, 64), jnp.bfloat16)], axis=1
    )
    mine[CROWS:, LATENT:] = jnp.concatenate(
        [span_ref[:, LATENT:], jnp.zeros((TOK, 64), jnp.bfloat16)], axis=1
    )

    def slot(zp, qp):
        return keys.at[zp, pl.ds(pl.multiple_of(c * HALF + qp * SHARD, SHARD), SHARD)]

    has_primary = (c == 1) | (q == x)

    @pl.when(has_primary)
    def _():
        slot(z, lead)[...] = mine[...]

    pl.semaphore_wait(barrier, 2 + 1 + 3 + 3 + 4 + 4 - selfs)

    def at(k):
        return (z + 8 + jnp.where(k % 2 == 1, -((k + 1) // 2), k // 2)) % 8

    def pre(n):
        d = (1, 2, 7)[n]
        return copy(mine, slot(z, x), s_pre.at[n], r_ring.at[z], device(x, (y + d) % 8, z, c))

    sends_pre = (c == 0) & (q == x)

    @pl.when(sends_pre)
    def _():
        for n in range(3):
            pre(n).start()

    @pl.when(jnp.logical_not(has_primary))
    def _():
        pre(0).wait_recv()

    def ring_copy(buf, zp, sem, ssem, dev):
        return copy(buf, buf, ssem.at[sem], r_ring.at[zp], dev)

    def stage1(k):
        zp = at(k)
        piece = slot(zp, lead)
        up = ring_copy(piece, zp, k, s_ring, z_up)
        down = ring_copy(piece, zp, k, s_ring, z_down)
        first_down = ring_copy(piece, zp, 8, s_ring, z_down)

        @pl.when(k > 0)
        def _():
            up.wait_recv()

        @pl.when((k == 0) | ((k % 2 == 1) & (k < 7)))
        def _():
            up.start()

        @pl.when((k % 2 == 0) & (k > 0) & (k < 6))
        def _():
            down.start()

        @pl.when(k == 0)
        def _():
            first_down.start()

        for n, d in enumerate((1, 3, 2)):
            copy(piece, piece, s_leaf.at[3 * k + n], r_leaf.at[zp * 4 + lead], leaf(d)).start()

    def half(zp, core):
        return keys.at[zp, pl.ds(pl.multiple_of(core * HALF, HALF), HALF)]

    def sib_copy(k):
        zp = at(k)
        return copy(half(zp, c), half(zp, c), s_sib.at[k], r_sib.at[zp], sibling)

    def stage2(k):
        zp = at(k)
        for d in (1, 3, 2):
            qp = (lead + d) % 4
            copy(slot(zp, qp), slot(zp, qp), s_leaf.at[0], r_leaf.at[zp * 4 + qp], leaf(1)).wait_recv()
        sib_copy(k).start()

    place = lax.broadcasted_iota(jnp.int32, (1, BLOCK), 1)
    core_of = jnp.where(place >= HALF, 1, 0)
    within = place - core_of * HALF
    plane = sum(jnp.where(within >= n * SHARD, 1, 0) for n in (1, 2, 3))
    row = within - plane * SHARD
    token_base = plane * 1024 + core_of * TOK + row - CROWS
    cache_base = plane * 256 + core_of * CROWS + row
    cached = row < CROWS
    length = length_ref[0]

    def flash(zp):
        code = jnp.where(
            cached,
            jnp.where(cache_base + zp * 32 < length, -1, FAR),
            token_base + zp * 128,
        )

        def chunk(i, carry):
            rows = pl.ds(pl.multiple_of(i * CHUNK, CHUNK), CHUNK)
            block = keys[zp]
            token = ctx * TOK + lax.broadcasted_iota(jnp.int32, (CHUNK, 1), 0) % TOK
            scores = lax.dot_general(
                queries[rows], block, (((1,), (1,)), ((), ())), preferred_element_type=jnp.float32
            )
            scores = jnp.where(code <= token, scores * SCALE2, MASKED)
            before = maxima[rows, :1]
            raised = jnp.maximum(before, jnp.max(scores, axis=1, keepdims=True))
            weights = jnp.exp2(scores - raised)
            factor = jnp.exp2(before - raised)
            maxima[rows] = jnp.broadcast_to(raised, (CHUNK, 128))
            totals[rows] = totals[rows] * factor + jnp.sum(weights, axis=1, keepdims=True)
            acc[rows] = acc[rows] * factor + jnp.dot(
                weights.astype(jnp.bfloat16), block[:, :LATENT], preferred_element_type=jnp.float32
            )
            return carry

        lax.fori_loop(0, ROWS // CHUNK, chunk, 0)

    stage1(0)

    for h in range(HEADS):
        nope = query_ref[:, h * 192 : h * 192 + NOPE]
        rope = query_ref[:, h * 192 + NOPE : (h + 1) * 192]
        absorbed = lax.dot_general(
            nope,
            kv_ref[:, h * 256 : h * 256 + NOPE],
            (((1,), (1,)), ((), ())),
            preferred_element_type=jnp.float32,
        ).astype(jnp.bfloat16)
        queries[h * TOK : (h + 1) * TOK, :LATENT] = absorbed
        queries[h * TOK : (h + 1) * TOK, LATENT:] = jnp.concatenate(
            [rope, jnp.zeros((TOK, 64), jnp.bfloat16)], axis=1
        )
    maxima[...] = jnp.full((ROWS, 128), MASKED, jnp.float32)
    totals[...] = jnp.zeros((ROWS, 128), jnp.float32)
    acc[...] = jnp.zeros((ROWS, LATENT), jnp.float32)

    def w_lanes(qp, core):
        return wbuf.at[:, pl.ds(pl.multiple_of(qp * 256 + core * 128, 128), 128)]

    w_lanes(q, c)[...] = jnp.concatenate(
        [w_ref[...], jnp.zeros((1024, 128 - COLS), jnp.bfloat16)], axis=1
    )

    stage1(1)
    stage1(2)

    def body(i, carry):
        for n in (3, 4):

            @pl.when(2 * i + n < 8)
            def _():
                stage1(2 * i + n)

        @pl.when(i < 8)
        def _():
            stage2(i)

        @pl.when(i > 0)
        def _():
            sib_copy(i - 1).wait_recv()
            flash(at(i - 1))

        return carry

    lax.fori_loop(0, 3, body, 0)

    def w_copy(d):
        return copy(
            w_lanes(q, c), w_lanes(q, c), s_w.at[d - 1], r_w.at[q * 2 + c], device(x, yh * 4 + (q + d) % 4, z, c)
        )

    for d in (1, 2, 3):
        w_copy(d).start()

    lax.fori_loop(3, 9, body, 0)

    latent_out[...] = (acc[...] / totals[:, :1]).astype(jnp.bfloat16)
    for h in range(HEADS):
        att[z, :, h * VDIM : (h + 1) * VDIM] = jnp.dot(
            latent_out[h * TOK : (h + 1) * TOK],
            kv_ref[:, h * 256 + NOPE : (h + 1) * 256],
            preferred_element_type=jnp.float32,
        ).astype(jnp.bfloat16)

    def att_copy(zp, n, dev):
        return copy(att.at[zp], att.at[zp], s_att.at[n], r_att.at[zp], dev)

    att_copy(z, 0, z_up).start()
    att_copy(z, 7, z_down).start()

    def w_sib(qp):
        return copy(w_lanes(qp, c), w_lanes(qp, c), s_wsib.at[qp], r_w.at[qp * 2 + c], sibling)

    for d in (1, 2, 3):
        qp = (q + d) % 4
        copy(w_lanes(qp, c), w_lanes(qp, c), s_w.at[0], r_w.at[qp * 2 + c], sibling).wait_recv()
    for qp in range(4):
        w_sib(qp).start()
    for qp in range(4):
        copy(w_lanes(qp, 1 - c), w_lanes(qp, 1 - c), s_w.at[0], r_w.at[qp * 2 + 1 - c], sibling).wait_recv()

    def collector(zp, pair):
        j = zp // 4
        return (x0 + jnp.where(pair == 0, j, 3 - j)) % 4

    def x_copy(zp, pair):
        r = collector(zp, pair)
        return r, copy(
            part.at[zp, :, pl.ds(pair * 512, 512)],
            landed.at[x, zp % 4],
            s_x.at[zp * 2 + pair],
            r_x.at[x * 4 + zp % 4],
            device(r, y, z, c),
        )

    def project(zp):
        part[zp] = jnp.dot(att[zp], wbuf[...], preferred_element_type=jnp.float32).astype(jnp.bfloat16)
        for pair in (0, 1):
            r, cp = x_copy(zp, pair)

            @pl.when(r != x)
            def _():
                cp.start()

    def out_step(k, carry):
        zp = at(k)

        @pl.when(k > 0)
        def _():
            att_copy(zp, k, z_up).wait_recv()

        @pl.when((k % 2 == 1) & (k < 7))
        def _():
            att_copy(zp, k, z_up).start()

        @pl.when((k % 2 == 0) & (k > 0) & (k < 6))
        def _():
            att_copy(zp, k, z_down).start()

        project(zp)
        return carry

    lax.fori_loop(0, 8, out_step, 0)

    def reduce_step(k, carry):
        zp = at(k)
        zi = zp % 4

        @pl.when(zp // 4 == my_j)
        def _():
            lanes = pl.ds(pl.multiple_of(my_pair * 512, 512), 512)
            total = part[zp, :, lanes].astype(jnp.float32)
            for d in (1, 2, 3):
                xs = (x + d) % 4
                copy(landed.at[xs, zi], landed.at[xs, zi], s_x.at[0], r_x.at[xs * 4 + zi], sibling).wait_recv()
                total = total + landed[xs, zi].astype(jnp.float32)
            reduced[pl.ds(pl.multiple_of(zi * TOK, TOK), TOK)] = total.astype(jnp.bfloat16)

        return carry

    lax.fori_loop(0, 8, reduce_step, 0)

    me_slot = yh * 2 + c
    for b in range(4):
        dx, dy, dc = target(b)
        src = reduced.at[:, pl.ds(b * 128, 128)]
        dst = final.at[me_slot]

        @pl.when(is_me(dx, dy, dc))
        def _():
            pltpu.make_async_copy(src, dst, r_f.at[me_slot]).start()

        @pl.when(jnp.logical_not(is_me(dx, dy, dc)))
        def _():
            copy(src, dst, s_f.at[b], r_f.at[me_slot], device(dx, dy, z, dc)).start()

    for core in range(2):
        for h in range(2):
            n = h * 2 + core
            copy(final.at[n], final.at[n], s_f.at[0], r_f.at[n], sibling).wait_recv()
        total = final[core].astype(jnp.float32) + final[2 + core].astype(jnp.float32)
        total = total[:, :COLS].astype(jnp.bfloat16)
        for zi in range(4):
            out_ref[zi * 128 + core * TOK : zi * 128 + (core + 1) * TOK] = total[zi * TOK : (zi + 1) * TOK]

    @pl.when(sends_pre)
    def _():
        for n in range(3):
            pre(n).wait_send()

    piece = slot(z, lead)
    for k in (0, 1, 2, 3, 4, 5, 8):
        copy(piece, piece, s_ring.at[k], r_ring.at[z], z_up).wait_send()
    for k in range(24):
        copy(piece, piece, s_leaf.at[k], r_ring.at[z], z_up).wait_send()
    for k in range(8):
        sib_copy(k).wait_send()
    for d in (1, 2, 3):
        w_copy(d).wait_send()
    for qp in range(4):
        w_sib(qp).wait_send()
    for n in (0, 1, 2, 3, 4, 5, 7):
        att_copy(z, n, z_up).wait_send()
    for zp in range(8):
        for pair in (0, 1):
            r, cp = x_copy(zp, pair)

            @pl.when(r != x)
            def _():
                cp.wait_send()

    for b in range(4):
        dx, dy, dc = target(b)

        @pl.when(jnp.logical_not(is_me(dx, dy, dc)))
        def _():
            copy(
                reduced.at[:, pl.ds(b * 128, 128)], final.at[me_slot], s_f.at[b], r_f.at[me_slot], sibling
            ).wait_send()


def on_device(span_query, span_latent, cache_latent, cache_length, kv_up_weight, out_weight):
    vmem = pl.BlockSpec(memory_space=pltpu.VMEM)
    dma = pltpu.SemaphoreType.DMA
    return pl.pallas_call(
        kernel,
        out_shape=jax.ShapeDtypeStruct((512, COLS), jnp.bfloat16),
        in_specs=[vmem, vmem, vmem, pl.BlockSpec(memory_space=pltpu.SMEM), vmem, vmem],
        out_specs=vmem,
        scratch_shapes=[
            pltpu.VMEM((8, BLOCK, WIDE), jnp.bfloat16),
            pltpu.VMEM((SHARD, WIDE), jnp.bfloat16),
            pltpu.VMEM((ROWS, WIDE), jnp.bfloat16),
            pltpu.VMEM((ROWS, 128), jnp.float32),
            pltpu.VMEM((ROWS, 128), jnp.float32),
            pltpu.VMEM((ROWS, LATENT), jnp.float32),
            pltpu.VMEM((ROWS, LATENT), jnp.bfloat16),
            pltpu.VMEM((1024, 1024), jnp.bfloat16),
            pltpu.VMEM((8, TOK, 1024), jnp.bfloat16),
            pltpu.VMEM((8, TOK, 1024), jnp.bfloat16),
            pltpu.VMEM((4, 4, TOK, 512), jnp.bfloat16),
            pltpu.VMEM((4 * TOK, 512), jnp.bfloat16),
            pltpu.VMEM((4, 4 * TOK, 128), jnp.bfloat16),
            dma((3,)),
            dma((9,)),
            dma((24,)),
            dma((8,)),
            dma((3,)),
            dma((4,)),
            dma((8,)),
            dma((16,)),
            dma((4,)),
            dma((8,)),
            dma((32,)),
            dma((8,)),
            dma((8,)),
            dma((8,)),
            dma((16,)),
            dma((4,)),
        ],
        compiler_params=pltpu.CompilerParams(
            collective_id=0, has_side_effects=True, vmem_limit_bytes=48 << 20
        ),
        cost_estimate=pl.CostEstimate(
            flops=8_000_000_000, bytes_accessed=4_000_000, transcendentals=2_600_000
        ),
        name="mla_prefill",
    )(span_query, span_latent, cache_latent, cache_length, kv_up_weight, out_weight)


def solution(mesh):
    return jax.shard_map(
        on_device,
        mesh=mesh,
        in_specs=(
            P("ctx", "head"),
            P("ctx", None),
            P("ctx", None),
            P(),
            P(None, "head"),
            P("head", "ctx"),
        ),
        out_specs=P("head", "ctx"),
        check_vma=False,
    )
```

time: 551 us -> 105 us (0.19)
  the two profiles are of different devices: /device:TPU:2 before, /device:TPU:55 now
where the time goes in v1:
time: 105 us
  Pallas kernels  98 us (93%)
  local copies, waits for them, and re-layouts  5.99 us (6%)
    pallas_call x1, Pallas kernels, on_device(): pl.pallas_call(kernel, out_shape=jax.ShapeDtypeStruct((512, COLS), jnp.bf...  98 us
    unnamed x9, local copies, waits for them, and re-layouts  5.23 us

profile of v1, /device:TPU:55, one launch (start us, length us, event | category | flops | bytes accessed | tf_op | source)
XLA Modules:
  0.0 104.7 jit_solution(5333371187011430693)
XLA Ops:
  0.7 1.1 %copy.7.w_ref = bf16[1024,112]{1,0:T(8,128)(2,1)S(1)} copy(bf16[1024,112]{0,1:T(8,128)(2,1)} %param.11) | data formatting | bytes 458752 | tf_op args[5]
  1.8 0.0 copy-start
  1.8 1.6 %copy-done = bf16[512,2048]{1,0:T(8,128)(2,1)S(1)} copy-done((bf16[512,2048]{1,0:T(8,128)(2,1)S(1)}, bf16[512,2048]{1,0:T(8,128)(2,1)}, u32[]{:S(2)}) %copy-start) | copy-done | bytes 2097176
  3.4 0.0 copy-start.1
  3.4 0.9 copy-done.1
  4.3 0.0 copy-start.2
  4.3 0.9 copy-done.2
  5.2 0.0 copy-start.3
  5.2 0.7 copy-done.3
  5.9 98.0 %mla_prefill.1 = bf16[512,112]{1,0:T(8,128)(2,1)S(1)} custom-call(bf16[64,1536]{1,0:T(8,128)(2,1)S(1)} %copy-done.1, bf16[64,576]{1,0:T(8,128)(2,1)S(1)} %copy-done.2, bf16[16,576]{1,0:T(8,128)(2,1)S(1)} %copy-done.3, s32[1]{0:T(128)S(6)} %copy.9.length_ref, bf16[512,2048]{1,0:T(8,128)(2,1)S(1)} %copy-done, bf16[1024,112]{1,0:T(8,128)(2,1)S(1)} %copy.7.w_ref), custom_call_target="tpu_custom_call" | custom-call | flops 8000000000 | bytes 4000000 | tf_op jit(solution)/shard_map/mla_prefill/pallas_call | solution.py:458
  103.9 0.8 copy.8
Async XLA Ops:
  1.8 1.6 %copy-start = (bf16[512,2048]{1,0:T(8,128)(2,1)S(1)}, bf16[512,2048]{1,0:T(8,128)(2,1)}, u32[]{:S(2)}) copy-start(bf16[512,2048]{1,0:T(8,128)(2,1)} %kv_ref.1) | copy-start | bytes 6291460
  3.4 0.9 copy-start.1
  4.3 0.9 copy-start.2
  5.2 0.7 copy-start.3

commit v2 on v1

v2 whole, which is shorter than its diff:
```python
import math

import jax
import jax.numpy as jnp
from jax import lax
from jax.experimental import pallas as pl
from jax.experimental.pallas import tpu as pltpu
from jax.sharding import PartitionSpec as P

LATENT = 512
ROPE = 64
NOPE = 128
VDIM = 128
HEADS = 8
TOK = 64
CROWS = 16
SHARD = TOK + CROWS
WIDE = 640
HALF = 4 * SHARD
BLOCK = 2 * HALF
COLS = 112
ROWS = HEADS * TOK
MASKED = -1e30
FAR = 1 << 30
MESH = pl.DeviceIdType.MESH
SCALE2 = (1.0 + 0.1 * math.log(40.0)) ** 2 / math.sqrt(NOPE + ROPE) * math.log2(math.e)


def kernel(
    query_hbm,
    span_hbm,
    cache_hbm,
    length_ref,
    kv_hbm,
    w_hbm,
    out_ref,
    query_ref,
    span_ref,
    cache_ref,
    kv_ref,
    keys,
    mine,
    queries,
    maxima,
    totals,
    acc,
    latent_out,
    wbuf,
    att,
    part,
    landed,
    reduced,
    final,
    s_in,
    s_pre,
    s_ring,
    s_leaf,
    s_sib,
    s_w,
    s_wsib,
    s_att,
    s_x,
    s_f,
    r_ring,
    r_leaf,
    r_sib,
    r_w,
    r_att,
    r_x,
    r_f,
):
    ctx = lax.axis_index("ctx")
    head = lax.axis_index("head")
    x, yh = head % 4, head // 4
    q, z, c = ctx // 16, (ctx // 2) % 8, ctx % 2
    y = yh * 4 + q

    def device(dx, dy, dz, dc):
        return {"ctx": ((dy % 4) * 8 + dz) * 2 + dc, "head": (dy // 4) * 4 + dx}

    z_up = device(x, y, (z + 1) % 8, c)
    z_down = device(x, y, (z + 7) % 8, c)
    sibling = device(x, y, z, 1 - c)
    lead = jnp.where(c == 0, x, q)
    two = jnp.where(q % 2 == 0, 2, 6)

    def leaf(delta):
        step = two if delta == 2 else (delta if delta == 1 else 7)
        return device(
            jnp.where(c == 0, (x + delta) % 4, x), jnp.where(c == 0, y, (y + step) % 8), z, c
        )

    x0 = 2 * (q % 2)
    role = (x - x0 + 4) % 4
    my_j = jnp.where((role == 1) | (role == 2), 1, 0)
    my_pair = role // 2

    def target(b):
        return x0 + my_j, 4 * (q // 2) + 2 * my_pair + b // 2, b % 2

    def is_me(dx, dy, dc):
        return (dx == x) & (dy == y) & (dc == c)

    def copy(src, dst, ssem, rsem, dev):
        return pltpu.make_async_remote_copy(
            src_ref=src, dst_ref=dst, send_sem=ssem, recv_sem=rsem, device_id=dev, device_id_type=MESH
        )

    def w_rows(qp, core):
        return wbuf.at[pl.ds(pl.multiple_of(qp * 256 + core * 128, 128), COLS)]

    loads = [
        pltpu.make_async_copy(src, dst, s_in.at[n])
        for n, (src, dst) in enumerate(
            (
                (span_hbm, span_ref),
                (cache_hbm, cache_ref),
                (query_hbm, query_ref),
                (kv_hbm, kv_ref),
                (w_hbm, w_rows(q, c)),
            )
        )
    ]
    for load in loads:
        load.start()

    barrier = pltpu.get_barrier_semaphore()

    def greet(dev):
        pl.semaphore_signal(barrier, inc=1, device_id=dev, device_id_type=MESH)

    greet(z_up)
    greet(z_down)
    greet(sibling)
    for d in (1, 2, 3):
        greet(device((x + d) % 4, y, z, c))
    for d in (1, 2, 6, 7):
        greet(device(x, (y + d) % 8, z, c))
    src_q = 2 * yh + x // 2
    src_j = x % 2
    src_x = jnp.where(q // 2 == 0, x, (2 * (x // 2) + 3 - src_j) % 4)
    for b in range(4):
        sx, sy, sc = src_x, src_q + 4 * (b // 2), b % 2

        @pl.when(jnp.logical_not(is_me(sx, sy, sc)))
        def _():
            greet(device(sx, sy, z, sc))

    selfs = 0
    for b in range(4):
        selfs = selfs + jnp.where(is_me(*target(b)), 1, 0)

    for n in range(8):
        wbuf[n * 128 + COLS : (n + 1) * 128] = jnp.zeros((128 - COLS, 1024), jnp.bfloat16)
    loads[0].wait()
    loads[1].wait()

    mine[:CROWS, :LATENT] = cache_ref[:, :LATENT]
    mine[CROWS:, :LATENT] = span_ref[:, :LATENT]
    mine[:CROWS, LATENT:] = jnp.concatenate(
        [cache_ref[:, LATENT:], jnp.zeros((CROWS, 64), jnp.bfloat16)], axis=1
    )
    mine[CROWS:, LATENT:] = jnp.concatenate(
        [span_ref[:, LATENT:], jnp.zeros((TOK, 64), jnp.bfloat16)], axis=1
    )

    def slot(zp, qp):
        return keys.at[zp, pl.ds(pl.multiple_of(c * HALF + qp * SHARD, SHARD), SHARD)]

    has_primary = (c == 1) | (q == x)

    @pl.when(has_primary)
    def _():
        slot(z, lead)[...] = mine[...]

    pl.semaphore_wait(barrier, 2 + 1 + 3 + 4 + 4 - selfs)

    def at(k):
        return (z + 8 + jnp.where(k % 2 == 1, -((k + 1) // 2), k // 2)) % 8

    def pre(n):
        d = (1, 2, 7)[n]
        return copy(mine, slot(z, x), s_pre.at[n], r_ring.at[z * 4 + x], device(x, (y + d) % 8, z, c))

    sends_pre = (c == 0) & (q == x)

    @pl.when(sends_pre)
    def _():
        for n in range(3):
            pre(n).start()

    @pl.when(jnp.logical_not(has_primary))
    def _():
        pre(0).wait_recv()

    def ring_copy(k, qp, sem, dev):
        piece = slot(at(k), qp)
        return copy(piece, piece, s_ring.at[sem], r_ring.at[at(k) * 4 + qp], dev)

    def leaf_copy(k, n):
        piece = slot(at(k), lead)
        d = (1, 3, 2)[n]
        return copy(piece, piece, s_leaf.at[3 * k + n], r_leaf.at[at(k) * 4 + lead], leaf(d))

    def leaf_wait(k, d):
        qp = (lead + d) % 4
        piece = slot(at(k), qp)
        copy(piece, piece, s_leaf.at[0], r_leaf.at[at(k) * 4 + qp], leaf(1)).wait_recv()
        return qp

    def forward(k, qp, low, high):
        ring_copy(k, qp, 0, z_up).wait_recv()

        @pl.when((k % 2 == 1) & ((k < 5) | (low & (k == 5))))
        def _():
            ring_copy(k, qp, 4 * k + qp, z_up).start()

        @pl.when((k % 2 == 0) & ((k < 6) | (high & (k == 6))))
        def _():
            ring_copy(k, qp, 4 * k + qp, z_down).start()

    def first(qp):
        ring_copy(0, qp, qp, z_up).start()
        ring_copy(0, qp, 28 + qp, z_down).start()

    def stage1(k):
        @pl.when(c == 0)
        def _():
            forward(k, lead, True, False)
            for n in range(3):
                leaf_copy(k, n).start()

        @pl.when(c == 1)
        def _():
            for qp in range(4):
                forward(k, qp, qp < 2, qp >= 2)
            sib_copy(k).start()

    def half(zp, core):
        return keys.at[zp, pl.ds(pl.multiple_of(core * HALF, HALF), HALF)]

    def sib_copy(k):
        zp = at(k)
        return copy(half(zp, c), half(zp, c), s_sib.at[k], r_sib.at[zp], sibling)

    def stage2(k):
        @pl.when(c == 0)
        def _():
            for d in (1, 3, 2):
                leaf_wait(k, d)
            sib_copy(k).start()

    place = lax.broadcasted_iota(jnp.int32, (1, BLOCK), 1)
    core_of = jnp.where(place >= HALF, 1, 0)
    within = place - core_of * HALF
    plane = sum(jnp.where(within >= n * SHARD, 1, 0) for n in (1, 2, 3))
    row = within - plane * SHARD
    token_base = plane * 1024 + core_of * TOK + row - CROWS
    cache_base = plane * 256 + core_of * CROWS + row
    cached = row < CROWS
    length = length_ref[0]

    def flash(zs, start, count):
        rows = pl.ds(start, count)
        token = ctx * TOK + lax.broadcasted_iota(jnp.int32, (count, 1), 0) % TOK
        scores = []
        for zp in zs:
            code = jnp.where(
                cached,
                jnp.where(cache_base + zp * 32 < length, -1, FAR),
                token_base + zp * 128,
            )
            product = lax.dot_general(
                queries[rows], keys[zp], (((1,), (1,)), ((), ())), preferred_element_type=jnp.float32
            )
            scores.append(jnp.where(code <= token, product * SCALE2, MASKED))
        before = maxima[rows, :1]
        raised = before
        for part_scores in scores:
            raised = jnp.maximum(raised, jnp.max(part_scores, axis=1, keepdims=True))
        factor = jnp.exp2(before - raised)
        maxima[rows] = jnp.broadcast_to(raised, (count, 128))
        total = totals[rows] * factor
        value = acc[rows] * factor
        for zp, part_scores in zip(zs, scores):
            weights = jnp.exp2(part_scores - raised)
            total = total + jnp.sum(weights, axis=1, keepdims=True)
            value = value + jnp.dot(
                weights.astype(jnp.bfloat16), keys[zp, :, :LATENT], preferred_element_type=jnp.float32
            )
        totals[rows] = total
        acc[rows] = value

    first(lead)
    for n in range(3):
        leaf_copy(0, n).start()

    def w_move(qp, sem, dev):
        return copy(w_rows(qp, c), w_rows(qp, c), s_w.at[sem], r_w.at[qp * 2 + c], dev)

    def w_sib(qp):
        return copy(w_rows(qp, c), w_rows(qp, c), s_wsib.at[qp], r_w.at[qp * 2 + c], sibling)

    def w_wait(qp, core):
        copy(w_rows(qp, core), w_rows(qp, core), s_w.at[0], r_w.at[qp * 2 + core], sibling).wait_recv()

    y_up = device(x, (y + 1) % 8, z, c)
    y_down = device(x, (y + 7) % 8, z, c)

    def w_round(n):
        @pl.when(q >= n)
        def _():
            if n > 0:
                w_wait(q - n, c)
                w_sib(q - n).start()

            @pl.when(q < 3)
            def _():
                w_move(q - n, n, y_up).start()

        @pl.when(q + n < 4)
        def _():
            if n > 0:
                w_wait(q + n, c)
                w_sib(q + n).start()

            @pl.when(q > 0)
            def _():
                w_move(q + n, 3 + n, y_down).start()

    loads[4].wait()
    w_round(0)
    w_sib(q).start()
    loads[2].wait()
    loads[3].wait()

    for h in range(HEADS):
        nope = query_ref[:, h * 192 : h * 192 + NOPE]
        rope = query_ref[:, h * 192 + NOPE : (h + 1) * 192]
        absorbed = lax.dot_general(
            nope,
            kv_ref[:, h * 256 : h * 256 + NOPE],
            (((1,), (1,)), ((), ())),
            preferred_element_type=jnp.float32,
        ).astype(jnp.bfloat16)
        queries[h * TOK : (h + 1) * TOK, :LATENT] = absorbed
        queries[h * TOK : (h + 1) * TOK, LATENT:] = jnp.concatenate(
            [rope, jnp.zeros((TOK, 64), jnp.bfloat16)], axis=1
        )
    maxima[...] = jnp.full((ROWS, 128), MASKED, jnp.float32)
    totals[...] = jnp.zeros((ROWS, 128), jnp.float32)
    acc[...] = jnp.zeros((ROWS, LATENT), jnp.float32)

    @pl.when(c == 1)
    def _():
        for d in (1, 3, 2):
            first(leaf_wait(0, d))
        sib_copy(0).start()

    def body(j, carry):
        for n in (0, 1):
            k = 2 * j + 1 + n

            @pl.when(k < 8)
            def _():
                stage1(k)

        @pl.when(j == 1)
        def _():
            sib_copy(0).wait_recv()
            flash([z], 0, ROWS)

        @pl.when(j > 1)
        def _():
            ks = (2 * j - 3, 2 * j - 2)
            for k in ks:
                sib_copy(k).wait_recv()
            flash([at(k) for k in ks], 0, ROWS)

        for n in (0, 1):
            k = 2 * j - 1 + n

            @pl.when((k >= 0) & (k < 8))
            def _():
                stage2(k)

        @pl.when(j == 2)
        def _():
            w_round(1)

        @pl.when(j == 3)
        def _():
            w_round(2)

        return carry

    lax.fori_loop(0, 5, body, 0)

    def att_copy(k, hf, sem, dev):
        piece = att.at[at(k), :, pl.ds(hf * 512, 512)]
        return copy(piece, piece, s_att.at[sem], r_att.at[at(k) * 2 + hf], dev)

    sib_copy(7).wait_recv()
    for hf in (0, 1):
        rows = pl.ds(hf * 256, 256)
        flash([at(7)], hf * 256, 256)
        latent_out[rows] = (acc[rows] / totals[rows, :1]).astype(jnp.bfloat16)
        for h in range(4 * hf, 4 * hf + 4):
            att[z, :, h * VDIM : (h + 1) * VDIM] = jnp.dot(
                latent_out[h * TOK : (h + 1) * TOK],
                kv_ref[:, h * 256 + NOPE : (h + 1) * 256],
                preferred_element_type=jnp.float32,
            ).astype(jnp.bfloat16)
        att_copy(0, hf, hf, z_up).start()
        att_copy(0, hf, 14 + hf, z_down).start()

    @pl.when(q == 3)
    def _():
        w_wait(0, c)
        w_sib(0).start()

    @pl.when(q == 0)
    def _():
        w_wait(3, c)
        w_sib(3).start()

    for qp in range(4):
        w_wait(qp, 1 - c)

    def collector(zp, pair):
        j = zp // 4
        return (x0 + jnp.where(pair == 0, j, 3 - j)) % 4

    def x_copy(zp, pair):
        r = collector(zp, pair)
        return r, copy(
            part.at[zp, :, pl.ds(pair * 512, 512)],
            landed.at[x, zp % 4],
            s_x.at[zp * 2 + pair],
            r_x.at[x * 4 + zp % 4],
            device(r, y, z, c),
        )

    def project(zs):
        rows = jnp.concatenate([att[zp] for zp in zs], axis=0)
        product = lax.dot_general(
            rows, wbuf[...], (((1,), (1,)), ((), ())), preferred_element_type=jnp.float32
        ).astype(jnp.bfloat16)
        for n, zp in enumerate(zs):
            part[zp] = product[n * TOK : (n + 1) * TOK]
            for pair in (0, 1):
                r, cp = x_copy(zp, pair)

                @pl.when(r != x)
                def _():
                    cp.start()

    me_slot = yh * 2 + c

    def final_parts(b, zi):
        rows = pl.ds(pl.multiple_of(zi * TOK, TOK), TOK)
        return reduced.at[rows, pl.ds(b * 128, 128)], final.at[me_slot, rows]

    def final_copy(b, zi):
        dx, dy, dc = target(b)
        src, dst = final_parts(b, zi)
        return copy(src, dst, s_f.at[b * 4 + zi], r_f.at[me_slot * 4 + zi], device(dx, dy, z, dc))

    def reduce(k):
        zp = at(k)
        zi = zp % 4

        @pl.when(zp // 4 == my_j)
        def _():
            lanes = pl.ds(pl.multiple_of(my_pair * 512, 512), 512)
            total = part[zp, :, lanes].astype(jnp.float32)
            for d in (1, 2, 3):
                xs = (x + d) % 4
                copy(landed.at[xs, zi], landed.at[xs, zi], s_x.at[0], r_x.at[xs * 4 + zi], sibling).wait_recv()
                total = total + landed[xs, zi].astype(jnp.float32)
            reduced[pl.ds(pl.multiple_of(zi * TOK, TOK), TOK)] = total.astype(jnp.bfloat16)
            for b in range(4):
                here = is_me(*target(b))

                @pl.when(here)
                def _():
                    src, dst = final_parts(b, zi)
                    pltpu.make_async_copy(src, dst, r_f.at[me_slot * 4 + zi]).start()

                @pl.when(jnp.logical_not(here))
                def _():
                    final_copy(b, zi).start()

    project([z])

    def out_step(j, carry):
        ks = (2 * j - 1, 2 * j)
        for k in ks:

            @pl.when(k < 8)
            def _():
                for hf in (0, 1):
                    att_copy(k, hf, 0, z_up).wait_recv()

                    @pl.when((k % 2 == 1) & ((k < 5) | ((k == 5) & (hf == 0))))
                    def _():
                        att_copy(k, hf, 2 * k + hf, z_up).start()

                    @pl.when((k % 2 == 0) & ((k < 6) | ((k == 6) & (hf == 1))))
                    def _():
                        att_copy(k, hf, 2 * k + hf, z_down).start()

        @pl.when(j < 4)
        def _():
            project([at(k) for k in ks])

        @pl.when(j == 4)
        def _():
            project([at(7)])

        reduce(2 * j - 2)

        @pl.when(j > 1)
        def _():
            reduce(2 * j - 3)

        return carry

    lax.fori_loop(1, 5, out_step, 0)
    reduce(7)

    for core in range(2):
        for h in range(2):
            n = h * 2 + core
            for zi in range(4):
                dst = final.at[n, pl.ds(zi * TOK, TOK)]
                copy(dst, dst, s_f.at[0], r_f.at[n * 4 + zi], sibling).wait_recv()
        total = final[core].astype(jnp.float32) + final[2 + core].astype(jnp.float32)
        total = total[:, :COLS].astype(jnp.bfloat16)
        for zi in range(4):
            out_ref[zi * 128 + core * TOK : zi * 128 + (core + 1) * TOK] = total[zi * TOK : (zi + 1) * TOK]

    @pl.when(sends_pre)
    def _():
        for n in range(3):
            pre(n).wait_send()

    @pl.when(c == 0)
    def _():
        for k in range(6):
            ring_copy(0, lead, 4 * k + lead, z_up).wait_send()
        ring_copy(0, lead, 28 + lead, z_up).wait_send()
        for k in range(8):
            for n in range(3):
                leaf_copy(k, n).wait_send()

    @pl.when(c == 1)
    def _():
        for n in range(24):
            if n not in (22, 23):
                ring_copy(0, 0, n, z_up).wait_send()
        for n in (26, 27, 28, 29, 30, 31):
            ring_copy(0, 0, n, z_up).wait_send()
        for n in range(3):
            leaf_copy(0, n).wait_send()

    for k in range(8):
        sib_copy(k).wait_send()
    for n in range(3):

        @pl.when((q >= n) & (q < 3))
        def _():
            w_move(0, n, y_up).wait_send()

        @pl.when((q + n < 4) & (q > 0))
        def _():
            w_move(0, 3 + n, y_down).wait_send()

    for qp in range(4):
        w_sib(qp).wait_send()
    for n in range(16):
        if n not in (11, 12):
            att_copy(0, 0, n, z_up).wait_send()
    for zp in range(8):
        for pair in (0, 1):
            r, cp = x_copy(zp, pair)

            @pl.when(r != x)
            def _():
                cp.wait_send()

    for b in range(4):

        @pl.when(jnp.logical_not(is_me(*target(b))))
        def _():
            for zi in range(4):
                final_copy(b, zi).wait_send()


def on_device(span_query, span_latent, cache_latent, cache_length, kv_up_weight, out_weight):
    vmem = pl.BlockSpec(memory_space=pltpu.VMEM)
    hbm = pl.BlockSpec(memory_space=pltpu.HBM)
    dma = pltpu.SemaphoreType.DMA
    return pl.pallas_call(
        kernel,
        out_shape=jax.ShapeDtypeStruct((512, COLS), jnp.bfloat16),
        in_specs=[hbm, hbm, hbm, pl.BlockSpec(memory_space=pltpu.SMEM), hbm, hbm],
        out_specs=vmem,
        scratch_shapes=[
            pltpu.VMEM((TOK, HEADS * 192), jnp.bfloat16),
            pltpu.VMEM((TOK, LATENT + ROPE), jnp.bfloat16),
            pltpu.VMEM((CROWS, LATENT + ROPE), jnp.bfloat16),
            pltpu.VMEM((LATENT, HEADS * 256), jnp.bfloat16),
            pltpu.VMEM((8, BLOCK, WIDE), jnp.bfloat16),
            pltpu.VMEM((SHARD, WIDE), jnp.bfloat16),
            pltpu.VMEM((ROWS, WIDE), jnp.bfloat16),
            pltpu.VMEM((ROWS, 128), jnp.float32),
            pltpu.VMEM((ROWS, 128), jnp.float32),
            pltpu.VMEM((ROWS, LATENT), jnp.float32),
            pltpu.VMEM((ROWS, LATENT), jnp.bfloat16),
            pltpu.VMEM((1024, 1024), jnp.bfloat16),
            pltpu.VMEM((8, TOK, 1024), jnp.bfloat16),
            pltpu.VMEM((8, TOK, 1024), jnp.bfloat16),
            pltpu.VMEM((4, 4, TOK, 512), jnp.bfloat16),
            pltpu.VMEM((4 * TOK, 512), jnp.bfloat16),
            pltpu.VMEM((4, 4 * TOK, 128), jnp.bfloat16),
            dma((5,)),
            dma((3,)),
            dma((32,)),
            dma((24,)),
            dma((8,)),
            dma((6,)),
            dma((4,)),
            dma((16,)),
            dma((16,)),
            dma((16,)),
            dma((32,)),
            dma((32,)),
            dma((8,)),
            dma((8,)),
            dma((16,)),
            dma((16,)),
            dma((16,)),
        ],
        compiler_params=pltpu.CompilerParams(
            collective_id=0, has_side_effects=True, vmem_limit_bytes=63 << 20
        ),
        cost_estimate=pl.CostEstimate(
            flops=8_000_000_000, bytes_accessed=4_000_000, transcendentals=2_600_000
        ),
        name="mla_prefill",
    )(span_query, span_latent, cache_latent, cache_length, kv_up_weight, out_weight.T)


def solution(mesh):
    return jax.shard_map(
        on_device,
        mesh=mesh,
        in_specs=(
            P("ctx", "head"),
            P("ctx", None),
            P("ctx", None),
            P(),
            P(None, "head"),
            P("head", "ctx"),
        ),
        out_specs=P("head", "ctx"),
        check_vma=False,
    )
```

time: 105 us -> 88.3 us (0.84)
  the two profiles are of different devices: /device:TPU:55 before, /device:TPU:127 now
where the time goes in v2:
time: 88.3 us; the launch traced here: 88.2 us
  Pallas kernels  85.9 us (97%)
  local copies, waits for them, and re-layouts  1.65 us (2%)
    pallas_call x1, Pallas kernels, on_device(): pl.pallas_call(kernel, out_shape=jax.ShapeDtypeStruct((512, COLS), jnp.bf...  85.9 us

profile of v2, /device:TPU:127, one launch (start us, length us, event | category | flops | bytes accessed | tf_op | source)
XLA Modules:
  0.0 88.2 jit_solution(6305670740133514403)
XLA Ops:
  0.7 85.9 %mla_prefill.1 = bf16[512,112]{1,0:T(8,128)(2,1)} custom-call(bf16[64,1536]{1,0:T(8,128)(2,1)} %query_hbm.1, bf16[64,576]{1,0:T(8,128)(2,1)} %span_hbm.1, bf16[16,576]{1,0:T(8,128)(2,1)} %cache_hbm.1, s32[1]{0:T(128)S(6)} %copy.8.length_ref, bf16[512,2048]{1,0:T(8,128)(2,1)} %kv_hbm.1, bf16[112,1024]{1,0:T(8,128)(2,1)} %bitcast.1), custom_call_target="tpu_custom_call" | custom-call | flops 8000000000 | bytes 4000000 | tf_op jit(solution)/shard_map/mla_prefill/pallas_call | solution.py:604
  86.5 1.7 %copy.7 = bf16[512,112]{0,1:T(8,128)(2,1)} copy(bf16[512,112]{1,0:T(8,128)(2,1)} %mla_prefill.1) | data formatting | bytes 229376 | tf_op jit(solution)/shard_map/mla_prefill/pallas_call | solution.py:604

commit v3 on v2

--- a/solution.py
+++ b/solution.py
@@ -55,6 +55,7 @@
     s_pre,
     s_ring,
     s_leaf,
+    s_far,
     s_sib,
     s_w,
     s_wsib,
@@ -63,6 +64,7 @@
     s_f,
     r_ring,
     r_leaf,
+    r_far,
     r_sib,
     r_w,
     r_att,
@@ -71,32 +73,31 @@
 ):
     ctx = lax.axis_index("ctx")
     head = lax.axis_index("head")
-    x, yh = head % 4, head // 4
-    q, z, c = ctx // 16, (ctx // 2) % 8, ctx % 2
+    x, yh = (head & 3), (head >> 2)
+    q, z, c = (ctx >> 4), (((ctx >> 1)) & 7), (ctx & 1)
     y = yh * 4 + q
 
     def device(dx, dy, dz, dc):
-        return {"ctx": ((dy % 4) * 8 + dz) * 2 + dc, "head": (dy // 4) * 4 + dx}
-
-    z_up = device(x, y, (z + 1) % 8, c)
-    z_down = device(x, y, (z + 7) % 8, c)
+        return {"ctx": (((dy & 3)) * 8 + dz) * 2 + dc, "head": ((dy >> 2)) * 4 + dx}
+
+    z_up = device(x, y, ((z + 1) & 7), c)
+    z_down = device(x, y, ((z + 7) & 7), c)
     sibling = device(x, y, z, 1 - c)
     lead = jnp.where(c == 0, x, q)
-    two = jnp.where(q % 2 == 0, 2, 6)
 
     def leaf(delta):
-        step = two if delta == 2 else (delta if delta == 1 else 7)
+        step = 1 if delta == 1 else 7
         return device(
-            jnp.where(c == 0, (x + delta) % 4, x), jnp.where(c == 0, y, (y + step) % 8), z, c
+            jnp.where(c == 0, ((x + delta) & 3), x), jnp.where(c == 0, y, ((y + step) & 7)), z, c
         )
 
-    x0 = 2 * (q % 2)
-    role = (x - x0 + 4) % 4
+    x0 = 2 * ((q & 1))
+    role = ((x - x0 + 4) & 3)
     my_j = jnp.where((role == 1) | (role == 2), 1, 0)
-    my_pair = role // 2
+    my_pair = (role >> 1)
 
     def target(b):
-        return x0 + my_j, 4 * (q // 2) + 2 * my_pair + b // 2, b % 2
+        return x0 + my_j, 4 * ((q >> 1)) + 2 * my_pair + (b >> 1), (b & 1)
 
     def is_me(dx, dy, dc):
         return (dx == x) & (dy == y) & (dc == c)
@@ -129,18 +130,18 @@
     def greet(dev):
         pl.semaphore_signal(barrier, inc=1, device_id=dev, device_id_type=MESH)
 
-    greet(z_up)
-    greet(z_down)
+    for dev in (z_up, z_down):
+        greet(dev)
     greet(sibling)
     for d in (1, 2, 3):
-        greet(device((x + d) % 4, y, z, c))
+        greet(device(((x + d) & 3), y, z, c))
     for d in (1, 2, 6, 7):
-        greet(device(x, (y + d) % 8, z, c))
-    src_q = 2 * yh + x // 2
-    src_j = x % 2
-    src_x = jnp.where(q // 2 == 0, x, (2 * (x // 2) + 3 - src_j) % 4)
+        greet(device(x, ((y + d) & 7), z, c))
+    src_q = 2 * yh + (x >> 1)
+    src_j = (x & 1)
+    src_x = jnp.where((q >> 1) == 0, x, ((2 * ((x >> 1)) + 3 - src_j) & 3))
     for b in range(4):
-        sx, sy, sc = src_x, src_q + 4 * (b // 2), b % 2
+        sx, sy, sc = src_x, src_q + 4 * ((b >> 1)), (b & 1)
 
         @pl.when(jnp.logical_not(is_me(sx, sy, sc)))
         def _():
@@ -176,11 +177,11 @@
     pl.semaphore_wait(barrier, 2 + 1 + 3 + 4 + 4 - selfs)
 
     def at(k):
-        return (z + 8 + jnp.where(k % 2 == 1, -((k + 1) // 2), k // 2)) % 8
+        return (z + 8 + jnp.where((k & 1) == 1, -(((k + 1) >> 1)), (k >> 1))) % 8
 
     def pre(n):
         d = (1, 2, 7)[n]
-        return copy(mine, slot(z, x), s_pre.at[n], r_ring.at[z * 4 + x], device(x, (y + d) % 8, z, c))
+        return copy(mine, slot(z, x), s_pre.at[n], r_ring.at[z * 4 + x], device(x, ((y + d) & 7), z, c))
 
     sends_pre = (c == 0) & (q == x)
 
@@ -199,11 +200,11 @@
 
     def leaf_copy(k, n):
         piece = slot(at(k), lead)
-        d = (1, 3, 2)[n]
+        d = (1, 3)[n]
         return copy(piece, piece, s_leaf.at[3 * k + n], r_leaf.at[at(k) * 4 + lead], leaf(d))
 
     def leaf_wait(k, d):
-        qp = (lead + d) % 4
+        qp = ((lead + d) & 3)
         piece = slot(at(k), qp)
         copy(piece, piece, s_leaf.at[0], r_leaf.at[at(k) * 4 + qp], leaf(1)).wait_recv()
         return qp
@@ -211,11 +212,11 @@
     def forward(k, qp, low, high):
         ring_copy(k, qp, 0, z_up).wait_recv()
 
-        @pl.when((k % 2 == 1) & ((k < 5) | (low & (k == 5))))
+        @pl.when(((k & 1) == 1) & ((k < 5) | (low & (k == 5))))
         def _():
             ring_copy(k, qp, 4 * k + qp, z_up).start()
 
-        @pl.when((k % 2 == 0) & ((k < 6) | (high & (k == 6))))
+        @pl.when(((k & 1) == 0) & ((k < 6) | (high & (k == 6))))
         def _():
             ring_copy(k, qp, 4 * k + qp, z_down).start()
 
@@ -224,17 +225,9 @@
         ring_copy(0, qp, 28 + qp, z_down).start()
 
     def stage1(k):
-        @pl.when(c == 0)
-        def _():
-            forward(k, lead, True, False)
-            for n in range(3):
-                leaf_copy(k, n).start()
-
-        @pl.when(c == 1)
-        def _():
-            for qp in range(4):
-                forward(k, qp, qp < 2, qp >= 2)
-            sib_copy(k).start()
+        forward(k, lead, True, False)
+        for n in range(2):
+            leaf_copy(k, n).start()
 
     def half(zp, core):
         return keys.at[zp, pl.ds(pl.multiple_of(core * HALF, HALF), HALF)]
@@ -243,12 +236,22 @@
         zp = at(k)
         return copy(half(zp, c), half(zp, c), s_sib.at[k], r_sib.at[zp], sibling)
 
+    def pass_copy(k, n, qp):
+        start, rows = ((0, 48), (48, 32))[n]
+        first_row = pl.multiple_of(c * HALF + qp * SHARD, SHARD) + start
+        piece = keys.at[at(k), pl.ds(first_row, rows)]
+        sem = (r_leaf.at[at(k) * 4 + qp], r_far.at[at(k)])[n]
+        return copy(piece, piece, s_far.at[2 * k + n], sem, leaf((3, 1)[n]))
+
     def stage2(k):
-        @pl.when(c == 0)
-        def _():
-            for d in (1, 3, 2):
-                leaf_wait(k, d)
-            sib_copy(k).start()
+        for n, d in enumerate((1, 3)):
+            qp = leaf_wait(k, d)
+            pass_copy(k, n, qp).start()
+
+    def stage3(k):
+        for n in range(2):
+            pass_copy(k, n, (lead + 2) & 3).wait_recv()
+        sib_copy(k).start()
 
     place = lax.broadcasted_iota(jnp.int32, (1, BLOCK), 1)
     core_of = jnp.where(place >= HALF, 1, 0)
@@ -262,7 +265,7 @@
 
     def flash(zs, start, count):
         rows = pl.ds(start, count)
-        token = ctx * TOK + lax.broadcasted_iota(jnp.int32, (count, 1), 0) % TOK
+        token = ctx * TOK + (lax.broadcasted_iota(jnp.int32, (count, 1), 0) & (TOK - 1))
         scores = []
         for zp in zs:
             code = jnp.where(
@@ -292,7 +295,7 @@
         acc[rows] = value
 
     first(lead)
-    for n in range(3):
+    for n in range(2):
         leaf_copy(0, n).start()
 
     def w_move(qp, sem, dev):
@@ -304,8 +307,8 @@
     def w_wait(qp, core):
         copy(w_rows(qp, core), w_rows(qp, core), s_w.at[0], r_w.at[qp * 2 + core], sibling).wait_recv()
 
-    y_up = device(x, (y + 1) % 8, z, c)
-    y_down = device(x, (y + 7) % 8, z, c)
+    y_up = device(x, ((y + 1) & 7), z, c)
+    y_down = device(x, ((y + 7) & 7), z, c)
 
     def w_round(n):
         @pl.when(q >= n)
@@ -351,40 +354,51 @@
     totals[...] = jnp.zeros((ROWS, 128), jnp.float32)
     acc[...] = jnp.zeros((ROWS, LATENT), jnp.float32)
 
-    @pl.when(c == 1)
-    def _():
-        for d in (1, 3, 2):
-            first(leaf_wait(0, d))
-        sib_copy(0).start()
-
-    def body(j, carry):
-        for n in (0, 1):
-            k = 2 * j + 1 + n
-
-            @pl.when(k < 8)
+    def pair_of(g, stage):
+        for k in (2 * g - 1, 2 * g):
+
+            @pl.when((k >= 0) & (k < 8))
             def _():
-                stage1(k)
-
-        @pl.when(j == 1)
+                stage(k)
+
+    def attend(g):
+        @pl.when(g == 0)
         def _():
             sib_copy(0).wait_recv()
             flash([z], 0, ROWS)
 
-        @pl.when(j > 1)
-        def _():
-            ks = (2 * j - 3, 2 * j - 2)
+        @pl.when(g > 0)
+        def _():
+            ks = (2 * g - 1, 2 * g)
             for k in ks:
                 sib_copy(k).wait_recv()
             flash([at(k) for k in ks], 0, ROWS)
 
-        for n in (0, 1):
-            k = 2 * j - 1 + n
-
-            @pl.when((k >= 0) & (k < 8))
-            def _():
-                stage2(k)
-
-        @pl.when(j == 2)
+    def w_last():
+        @pl.when(q == 3)
+        def _():
+            w_wait(0, c)
+            w_sib(0).start()
+
+        @pl.when(q == 0)
+        def _():
+            w_wait(3, c)
+            w_sib(3).start()
+
+    def body(j, carry):
+        @pl.when(j < 4)
+        def _():
+            pair_of(j + 1, stage1)
+
+        @pl.when(j < 5)
+        def _():
+            pair_of(j, stage2)
+
+        @pl.when(j > 0)
+        def _():
+            pair_of(j - 1, stage3)
+
+        @pl.when(j == 1)
         def _():
             w_round(1)
 
@@ -392,9 +406,17 @@
         def _():
             w_round(2)
 
+        @pl.when(j == 5)
+        def _():
+            w_last()
+
+        @pl.when(j > 1)
+        def _():
+            attend(j - 2)
+
         return carry
 
-    lax.fori_loop(0, 5, body, 0)
+    lax.fori_loop(0, 6, body, 0)
 
     def att_copy(k, hf, sem, dev):
         piece = att.at[at(k), :, pl.ds(hf * 512, 512)]
@@ -414,30 +436,20 @@
         att_copy(0, hf, hf, z_up).start()
         att_copy(0, hf, 14 + hf, z_down).start()
 
-    @pl.when(q == 3)
-    def _():
-        w_wait(0, c)
-        w_sib(0).start()
-
-    @pl.when(q == 0)
-    def _():
-        w_wait(3, c)
-        w_sib(3).start()
-
     for qp in range(4):
         w_wait(qp, 1 - c)
 
     def collector(zp, pair):
-        j = zp // 4
-        return (x0 + jnp.where(pair == 0, j, 3 - j)) % 4
+        j = (zp >> 2)
+        return ((x0 + jnp.where(pair == 0, j, 3 - j)) & 3)
 
     def x_copy(zp, pair):
         r = collector(zp, pair)
         return r, copy(
             part.at[zp, :, pl.ds(pair * 512, 512)],
-            landed.at[x, zp % 4],
+            landed.at[x, (zp & 3)],
             s_x.at[zp * 2 + pair],
-            r_x.at[x * 4 + zp % 4],
+            r_x.at[x * 4 + (zp & 3)],
             device(r, y, z, c),
         )
 
@@ -468,14 +480,14 @@
 
     def reduce(k):
         zp = at(k)
-        zi = zp % 4
-
-        @pl.when(zp // 4 == my_j)
+        zi = (zp & 3)
+
+        @pl.when((zp >> 2) == my_j)
         def _():
             lanes = pl.ds(pl.multiple_of(my_pair * 512, 512), 512)
             total = part[zp, :, lanes].astype(jnp.float32)
             for d in (1, 2, 3):
-                xs = (x + d) % 4
+                xs = ((x + d) & 3)
                 copy(landed.at[xs, zi], landed.at[xs, zi], s_x.at[0], r_x.at[xs * 4 + zi], sibling).wait_recv()
                 total = total + landed[xs, zi].astype(jnp.float32)
             reduced[pl.ds(pl.multiple_of(zi * TOK, TOK), TOK)] = total.astype(jnp.bfloat16)
@@ -502,11 +514,11 @@
                 for hf in (0, 1):
                     att_copy(k, hf, 0, z_up).wait_recv()
 
-                    @pl.when((k % 2 == 1) & ((k < 5) | ((k == 5) & (hf == 0))))
+                    @pl.when(((k & 1) == 1) & ((k < 5) | ((k == 5) & (hf == 0))))
                     def _():
                         att_copy(k, hf, 2 * k + hf, z_up).start()
 
-                    @pl.when((k % 2 == 0) & ((k < 6) | ((k == 6) & (hf == 1))))
+                    @pl.when(((k & 1) == 0) & ((k < 6) | ((k == 6) & (hf == 1))))
                     def _():
                         att_copy(k, hf, 2 * k + hf, z_down).start()
 
@@ -545,25 +557,13 @@
         for n in range(3):
             pre(n).wait_send()
 
-    @pl.when(c == 0)
-    def _():
-        for k in range(6):
-            ring_copy(0, lead, 4 * k + lead, z_up).wait_send()
-        ring_copy(0, lead, 28 + lead, z_up).wait_send()
-        for k in range(8):
-            for n in range(3):
-                leaf_copy(k, n).wait_send()
-
-    @pl.when(c == 1)
-    def _():
-        for n in range(24):
-            if n not in (22, 23):
-                ring_copy(0, 0, n, z_up).wait_send()
-        for n in (26, 27, 28, 29, 30, 31):
-            ring_copy(0, 0, n, z_up).wait_send()
-        for n in range(3):
-            leaf_copy(0, n).wait_send()
-
+    for k in range(6):
+        ring_copy(0, lead, 4 * k + lead, z_up).wait_send()
+    ring_copy(0, lead, 28 + lead, z_up).wait_send()
+    for k in range(8):
+        for n in range(2):
+            leaf_copy(k, n).wait_send()
+            pass_copy(k, n, lead).wait_send()
     for k in range(8):
         sib_copy(k).wait_send()
     for n in range(3):
@@ -628,6 +628,7 @@
             dma((3,)),
             dma((32,)),
             dma((24,)),
+            dma((16,)),
             dma((8,)),
             dma((6,)),
             dma((4,)),
@@ -636,6 +637,7 @@
             dma((16,)),
             dma((32,)),
             dma((32,)),
+            dma((8,)),
             dma((8,)),
             dma((8,)),
             dma((16,)),

time: 88.3 us -> 84.7 us (0.959)
  Pallas kernels: 85.9 us -> 82.3 us
    pallas_call x1, Pallas kernels: 85.9 us -> 82.3 us  [on_device(): pl.pallas_call(kernel, out_shape=jax.ShapeDtypeStruct((512, COLS), jnp.bf...]
where the time goes in v3:
time: 84.7 us; the launch traced here: 84.6 us
  Pallas kernels  82.3 us (97%)
  local copies, waits for them, and re-layouts  1.65 us (2%)
    pallas_call x1, Pallas kernels, on_device(): pl.pallas_call(kernel, out_shape=jax.ShapeDtypeStruct((512, COLS), jnp.bf...  82.3 us

profile of v3, /device:TPU:127, one launch (start us, length us, event | category | flops | bytes accessed | tf_op | source)
XLA Modules:
  0.0 84.6 jit_solution(4578945619917098916)
XLA Ops:
  0.7 82.3 %mla_prefill.1 = bf16[512,112]{1,0:T(8,128)(2,1)} custom-call(bf16[64,1536]{1,0:T(8,128)(2,1)} %query_hbm.1, bf16[64,576]{1,0:T(8,128)(2,1)} %span_hbm.1, bf16[16,576]{1,0:T(8,128)(2,1)} %cache_hbm.1, s32[1]{0:T(128)S(6)} %copy.8.length_ref, bf16[512,2048]{1,0:T(8,128)(2,1)} %kv_hbm.1, bf16[112,1024]{1,0:T(8,128)(2,1)} %bitcast.1), custom_call_target="tpu_custom_call" | custom-call | flops 8000000000 | bytes 4000000 | tf_op jit(solution)/shard_map/mla_prefill/pallas_call | solution.py:604
  82.9 1.7 %copy.7 = bf16[512,112]{0,1:T(8,128)(2,1)} copy(bf16[512,112]{1,0:T(8,128)(2,1)} %mla_prefill.1) | data formatting | bytes 229376 | tf_op jit(solution)/shard_map/mla_prefill/pallas_call | solution.py:604

commit v4 on v3

--- a/solution.py
+++ b/solution.py
@@ -1,3 +1,4 @@
+import functools
 import math
 
 import jax
@@ -50,7 +51,6 @@
     part,
     landed,
     reduced,
-    final,
     s_in,
     s_pre,
     s_ring,
@@ -64,7 +64,6 @@
     s_f,
     r_ring,
     r_leaf,
-    r_far,
     r_sib,
     r_w,
     r_att,
@@ -82,6 +81,8 @@
 
     z_up = device(x, y, ((z + 1) & 7), c)
     z_down = device(x, y, ((z + 7) & 7), c)
+    z_up2 = device(x, y, ((z + 2) & 7), c)
+    z_down2 = device(x, y, ((z + 6) & 7), c)
     sibling = device(x, y, z, 1 - c)
     lead = jnp.where(c == 0, x, q)
 
@@ -122,15 +123,12 @@
             )
         )
     ]
-    for load in loads:
-        load.start()
-
     barrier = pltpu.get_barrier_semaphore()
 
     def greet(dev):
         pl.semaphore_signal(barrier, inc=1, device_id=dev, device_id_type=MESH)
 
-    for dev in (z_up, z_down):
+    for dev in (z_up, z_down, z_up2, z_down2):
         greet(dev)
     greet(sibling)
     for d in (1, 2, 3):
@@ -147,6 +145,9 @@
         def _():
             greet(device(sx, sy, z, sc))
 
+    for load in loads:
+        load.start()
+
     selfs = 0
     for b in range(4):
         selfs = selfs + jnp.where(is_me(*target(b)), 1, 0)
@@ -174,60 +175,73 @@
     def _():
         slot(z, lead)[...] = mine[...]
 
-    pl.semaphore_wait(barrier, 2 + 1 + 3 + 4 + 4 - selfs)
+    pl.semaphore_wait(barrier, 4 + 1 + 3 + 4 + 4 - selfs)
 
     def at(k):
         return (z + 8 + jnp.where((k & 1) == 1, -(((k + 1) >> 1)), (k >> 1))) % 8
 
-    def pre(n):
-        d = (1, 2, 7)[n]
-        return copy(mine, slot(z, x), s_pre.at[n], r_ring.at[z * 4 + x], device(x, ((y + d) & 7), z, c))
+    parts = ((0, 48), (48, 32))
+
+    def piece_of(zp, qp, n):
+        start, rows = parts[n]
+        return keys.at[zp, pl.ds(pl.multiple_of(c * HALF + qp * SHARD, SHARD) + start, rows)]
+
+    def pre(m, n):
+        d = (1, 7, 2)[m]
+        start, rows = parts[n]
+        src = mine.at[pl.ds(start, rows)]
+        dev = device(x, ((y + d) & 7), z, c)
+        return copy(src, piece_of(z, x, n), s_pre.at[2 * m + n], r_ring.at[2 * z + n], dev)
 
     sends_pre = (c == 0) & (q == x)
 
     @pl.when(sends_pre)
     def _():
-        for n in range(3):
-            pre(n).start()
-
-    @pl.when(jnp.logical_not(has_primary))
-    def _():
-        pre(0).wait_recv()
-
-    def ring_copy(k, qp, sem, dev):
-        piece = slot(at(k), qp)
-        return copy(piece, piece, s_ring.at[sem], r_ring.at[at(k) * 4 + qp], dev)
-
-    def leaf_copy(k, n):
-        piece = slot(at(k), lead)
-        d = (1, 3)[n]
-        return copy(piece, piece, s_leaf.at[3 * k + n], r_leaf.at[at(k) * 4 + lead], leaf(d))
-
-    def leaf_wait(k, d):
-        qp = ((lead + d) & 3)
-        piece = slot(at(k), qp)
-        copy(piece, piece, s_leaf.at[0], r_leaf.at[at(k) * 4 + qp], leaf(1)).wait_recv()
+        for n in range(2):
+            for m in range(3):
+                pre(m, n).start()
+
+    def ring_copy(k, n, sem, dev):
+        piece = piece_of(at(k), lead, n)
+        return copy(piece, piece, s_ring.at[sem], r_ring.at[2 * at(k) + n], dev)
+
+    def leaf_copy(k, n, m):
+        piece = piece_of(at(k), lead, n)
+        d = (1, 3)[m]
+        sem = r_leaf.at[(at(k) * 4 + lead) * 2 + n]
+        return copy(piece, piece, s_leaf.at[4 * k + 2 * n + m], sem, leaf(d))
+
+    def leaf_wait(k, d, n):
+        qp = (lead + d) & 3
+        piece = piece_of(at(k), qp, n)
+        copy(piece, piece, s_leaf.at[0], r_leaf.at[(at(k) * 4 + qp) * 2 + n], sibling).wait_recv()
         return qp
 
-    def forward(k, qp, low, high):
-        ring_copy(k, qp, 0, z_up).wait_recv()
-
-        @pl.when(((k & 1) == 1) & ((k < 5) | (low & (k == 5))))
-        def _():
-            ring_copy(k, qp, 4 * k + qp, z_up).start()
-
-        @pl.when(((k & 1) == 0) & ((k < 6) | (high & (k == 6))))
-        def _():
-            ring_copy(k, qp, 4 * k + qp, z_down).start()
-
-    def first(qp):
-        ring_copy(0, qp, qp, z_up).start()
-        ring_copy(0, qp, 28 + qp, z_down).start()
-
-    def stage1(k):
-        forward(k, lead, True, False)
-        for n in range(2):
-            leaf_copy(k, n).start()
+    def leaves(k, n):
+        for m in range(2):
+            leaf_copy(k, n, m).start()
+
+    def first(n):
+        ring_copy(0, n, n, z_up).start()
+        ring_copy(0, n, 10 + n, z_down).start()
+        leaves(0, n)
+
+    def stage1(k, n):
+        ring_copy(k, n, 0, z_up).wait_recv()
+
+        @pl.when((k == 1) | (k == 3))
+        def _():
+            ring_copy(k, n, 2 * k + n, z_up).start()
+
+        @pl.when((k == 2) | (k == 4))
+        def _():
+            ring_copy(k, n, 2 * k + n, z_down).start()
+
+        @pl.when(k == 3 + n)
+        def _():
+            ring_copy(k, n, 12 + n, (z_up2, z_down2)[n]).start()
+
+        leaves(k, n)
 
     def half(zp, core):
         return keys.at[zp, pl.ds(pl.multiple_of(core * HALF, HALF), HALF)]
@@ -237,20 +251,18 @@
         return copy(half(zp, c), half(zp, c), s_sib.at[k], r_sib.at[zp], sibling)
 
     def pass_copy(k, n, qp):
-        start, rows = ((0, 48), (48, 32))[n]
-        first_row = pl.multiple_of(c * HALF + qp * SHARD, SHARD) + start
-        piece = keys.at[at(k), pl.ds(first_row, rows)]
-        sem = (r_leaf.at[at(k) * 4 + qp], r_far.at[at(k)])[n]
+        piece = piece_of(at(k), qp, n)
+        sem = r_leaf.at[(at(k) * 4 + qp) * 2 + n]
         return copy(piece, piece, s_far.at[2 * k + n], sem, leaf((3, 1)[n]))
 
     def stage2(k):
         for n, d in enumerate((1, 3)):
-            qp = leaf_wait(k, d)
-            pass_copy(k, n, qp).start()
+            pass_copy(k, n, leaf_wait(k, d, n)).start()
 
     def stage3(k):
-        for n in range(2):
-            pass_copy(k, n, (lead + 2) & 3).wait_recv()
+        for n, d in enumerate((3, 1)):
+            leaf_wait(k, d, n)
+            leaf_wait(k, 2, n)
         sib_copy(k).start()
 
     place = lax.broadcasted_iota(jnp.int32, (1, BLOCK), 1)
@@ -294,9 +306,14 @@
         totals[rows] = total
         acc[rows] = value
 
-    first(lead)
     for n in range(2):
-        leaf_copy(0, n).start()
+
+        @pl.when(jnp.logical_not(has_primary))
+        def _():
+            pre(0, n).wait_recv()
+
+        first(n)
+
 
     def w_move(qp, sem, dev):
         return copy(w_rows(qp, c), w_rows(qp, c), s_w.at[sem], r_w.at[qp * 2 + c], dev)
@@ -388,7 +405,8 @@
     def body(j, carry):
         @pl.when(j < 4)
         def _():
-            pair_of(j + 1, stage1)
+            for n in range(2):
+                pair_of(j + 1, functools.partial(stage1, n=n))
 
         @pl.when(j < 5)
         def _():
@@ -418,9 +436,9 @@
 
     lax.fori_loop(0, 6, body, 0)
 
-    def att_copy(k, hf, sem, dev):
-        piece = att.at[at(k), :, pl.ds(hf * 512, 512)]
-        return copy(piece, piece, s_att.at[sem], r_att.at[at(k) * 2 + hf], dev)
+    def att_copy(k, n, sem, dev):
+        piece = att.at[at(k), :, pl.ds(n * 256, 256)]
+        return copy(piece, piece, s_att.at[sem], r_att.at[at(k) * 4 + n], dev)
 
     sib_copy(7).wait_recv()
     for hf in (0, 1):
@@ -433,8 +451,9 @@
                 kv_ref[:, h * 256 + NOPE : (h + 1) * 256],
                 preferred_element_type=jnp.float32,
             ).astype(jnp.bfloat16)
-        att_copy(0, hf, hf, z_up).start()
-        att_copy(0, hf, 14 + hf, z_down).start()
+        for n in (2 * hf, 2 * hf + 1):
+            att_copy(0, n, n, z_up).start()
+            att_copy(0, n, 4 + n, z_down).start()
 
     for qp in range(4):
         w_wait(qp, 1 - c)
@@ -471,7 +490,8 @@
 
     def final_parts(b, zi):
         rows = pl.ds(pl.multiple_of(zi * TOK, TOK), TOK)
-        return reduced.at[rows, pl.ds(b * 128, 128)], final.at[me_slot, rows]
+        there = pl.ds(pl.multiple_of(zi * 128 + c * TOK, TOK), TOK)
+        return reduced.at[rows, pl.ds(b * 128, 128)], out_ref.at[yh, there]
 
     def final_copy(b, zi):
         dx, dy, dc = target(b)
@@ -505,31 +525,35 @@
 
     project([z])
 
+    def arrive(k):
+        for n in range(4):
+            att_copy(k, n, 0, z_up).wait_recv()
+
+            @pl.when((k == 1) | (k == 3))
+            def _():
+                att_copy(k, n, 4 * k + 4 + n, z_up).start()
+
+            @pl.when((k == 2) | (k == 4))
+            def _():
+                att_copy(k, n, 4 * k + 4 + n, z_down).start()
+
+            if n < 2:
+
+                @pl.when(k == 3)
+                def _():
+                    att_copy(k, n, 24 + n, z_up2).start()
+
+            else:
+
+                @pl.when(k == 4)
+                def _():
+                    att_copy(k, n, 24 + n, z_down2).start()
+
     def out_step(j, carry):
         ks = (2 * j - 1, 2 * j)
         for k in ks:
-
-            @pl.when(k < 8)
-            def _():
-                for hf in (0, 1):
-                    att_copy(k, hf, 0, z_up).wait_recv()
-
-                    @pl.when(((k & 1) == 1) & ((k < 5) | ((k == 5) & (hf == 0))))
-                    def _():
-                        att_copy(k, hf, 2 * k + hf, z_up).start()
-
-                    @pl.when(((k & 1) == 0) & ((k < 6) | ((k == 6) & (hf == 1))))
-                    def _():
-                        att_copy(k, hf, 2 * k + hf, z_down).start()
-
-        @pl.when(j < 4)
-        def _():
-            project([at(k) for k in ks])
-
-        @pl.when(j == 4)
-        def _():
-            project([at(7)])
-
+            arrive(k)
+        project([at(k) for k in ks])
         reduce(2 * j - 2)
 
         @pl.when(j > 1)
@@ -538,32 +562,30 @@
 
         return carry
 
-    lax.fori_loop(1, 5, out_step, 0)
-    reduce(7)
-
-    for core in range(2):
-        for h in range(2):
-            n = h * 2 + core
-            for zi in range(4):
-                dst = final.at[n, pl.ds(zi * TOK, TOK)]
-                copy(dst, dst, s_f.at[0], r_f.at[n * 4 + zi], sibling).wait_recv()
-        total = final[core].astype(jnp.float32) + final[2 + core].astype(jnp.float32)
-        total = total[:, :COLS].astype(jnp.bfloat16)
+    lax.fori_loop(1, 4, out_step, 0)
+    arrive(7)
+    project([at(7)])
+    for k in (5, 6, 7):
+        reduce(k)
+
+    for n in range(4):
         for zi in range(4):
-            out_ref[zi * 128 + core * TOK : zi * 128 + (core + 1) * TOK] = total[zi * TOK : (zi + 1) * TOK]
+            dst = out_ref.at[n // 2, pl.ds(zi * 128 + (n % 2) * TOK, TOK)]
+            copy(dst, dst, s_f.at[0], r_f.at[n * 4 + zi], sibling).wait_recv()
 
     @pl.when(sends_pre)
     def _():
-        for n in range(3):
-            pre(n).wait_send()
-
-    for k in range(6):
-        ring_copy(0, lead, 4 * k + lead, z_up).wait_send()
-    ring_copy(0, lead, 28 + lead, z_up).wait_send()
+        for n in range(2):
+            for m in range(3):
+                pre(m, n).wait_send()
+
+    for sem in range(14):
+        ring_copy(0, sem & 1, sem, z_up).wait_send()
     for k in range(8):
         for n in range(2):
-            leaf_copy(k, n).wait_send()
             pass_copy(k, n, lead).wait_send()
+            for m in range(2):
+                leaf_copy(k, n, m).wait_send()
     for k in range(8):
         sib_copy(k).wait_send()
     for n in range(3):
@@ -578,9 +600,8 @@
 
     for qp in range(4):
         w_sib(qp).wait_send()
-    for n in range(16):
-        if n not in (11, 12):
-            att_copy(0, 0, n, z_up).wait_send()
+    for n in range(28):
+        att_copy(0, 0, n, z_up).wait_send()
     for zp in range(8):
         for pair in (0, 1):
             r, cp = x_copy(zp, pair)
@@ -598,14 +619,13 @@
 
 
 def on_device(span_query, span_latent, cache_latent, cache_length, kv_up_weight, out_weight):
-    vmem = pl.BlockSpec(memory_space=pltpu.VMEM)
     hbm = pl.BlockSpec(memory_space=pltpu.HBM)
     dma = pltpu.SemaphoreType.DMA
-    return pl.pallas_call(
+    halves = pl.pallas_call(
         kernel,
-        out_shape=jax.ShapeDtypeStruct((512, COLS), jnp.bfloat16),
+        out_shape=jax.ShapeDtypeStruct((2, 512, 128), jnp.bfloat16),
         in_specs=[hbm, hbm, hbm, pl.BlockSpec(memory_space=pltpu.SMEM), hbm, hbm],
-        out_specs=vmem,
+        out_specs=hbm,
         scratch_shapes=[
             pltpu.VMEM((TOK, HEADS * 192), jnp.bfloat16),
             pltpu.VMEM((TOK, LATENT + ROPE), jnp.bfloat16),
@@ -623,24 +643,22 @@
             pltpu.VMEM((8, TOK, 1024), jnp.bfloat16),
             pltpu.VMEM((4, 4, TOK, 512), jnp.bfloat16),
             pltpu.VMEM((4 * TOK, 512), jnp.bfloat16),
-            pltpu.VMEM((4, 4 * TOK, 128), jnp.bfloat16),
             dma((5,)),
-            dma((3,)),
+            dma((6,)),
+            dma((14,)),
             dma((32,)),
-            dma((24,)),
             dma((16,)),
             dma((8,)),
             dma((6,)),
             dma((4,)),
+            dma((28,)),
             dma((16,)),
             dma((16,)),
             dma((16,)),
-            dma((32,)),
-            dma((32,)),
+            dma((64,)),
             dma((8,)),
             dma((8,)),
-            dma((8,)),
-            dma((16,)),
+            dma((32,)),
             dma((16,)),
             dma((16,)),
         ],
@@ -652,6 +670,8 @@
         ),
         name="mla_prefill",
     )(span_query, span_latent, cache_latent, cache_length, kv_up_weight, out_weight.T)
+    total = halves[0].astype(jnp.float32) + halves[1].astype(jnp.float32)
+    return total[:, :COLS].astype(jnp.bfloat16)
 
 
 def solution(mesh):

time: 84.7 us -> 83.8 us (0.989)
  Pallas kernels: 82.3 us -> 81.2 us
  other arithmetic: 0 us -> 1.01 us
  local copies, waits for them, and re-layouts: 1.65 us -> 0.76 us
    pallas_call x1 -> x0, local copies, waits for them, and re-layouts: 1.65 us -> none  [on_device(): pl.pallas_call(kernel, out_shape=jax.ShapeDtypeStruct((512, COLS), jnp.bf...]
    pallas_call x1, Pallas kernels: 82.3 us -> 81.2 us  [on_device(): pl.pallas_call(kernel, out_shape=jax.ShapeDtypeStruct((2, 512, 128), jnp....]
    add x0 -> x1, other arithmetic: none -> 1.01 us  [on_device(): total = halves[0].astype(jnp.float32) + halves[1].astype(jnp.float32)]
where the time goes in v4:
time: 83.8 us; the launch traced here: 83.6 us
  Pallas kernels  81.2 us (97%)
  other arithmetic  1.01 us (1%)
    pallas_call x1, Pallas kernels, on_device(): pl.pallas_call(kernel, out_shape=jax.ShapeDtypeStruct((2, 512, 128), jnp....  81.2 us

profile of v4, /device:TPU:127, one launch (start us, length us, event | category | flops | bytes accessed | tf_op | source)
XLA Modules:
  0.0 83.6 jit_solution(5271570176384359184)
XLA Ops:
  0.7 81.2 %mla_prefill.1 = bf16[2,512,128]{2,1,0:T(8,128)(2,1)} custom-call(bf16[64,1536]{1,0:T(8,128)(2,1)} %query_hbm.1, bf16[64,576]{1,0:T(8,128)(2,1)} %span_hbm.1, bf16[16,576]{1,0:T(8,128)(2,1)} %cache_hbm.1, s32[1]{0:T(128)S(6)} %copy.8.length_ref, bf16[512,2048]{1,0:T(8,128)(2,1)} %kv_hbm.1, bf16[112,1024]{1,0:T(8,128)(2,1)} %bitcast.5), custom_call_target="tpu_custom_call" | custom-call | flops 8000000000 | bytes 4000000 | tf_op jit(solution)/shard_map/mla_prefill/pallas_call | solution.py:624
  81.9 1.0 %fusion = bf16[512,128]{1,0:T(8,128)(2,1)S(1)} fusion(bf16[2,512,128]{2,1,0:T(8,128)(2,1)} %mla_prefill.1), kind=kLoop, calls=%fused_computation.1 | loop fusion | flops 262144 | bytes 393216 | tf_op jit(solution)/shard_map/add | solution.py:673
  82.9 0.8 copy.7

commit v5 on v4

--- a/solution.py
+++ b/solution.py
@@ -276,35 +276,39 @@
     length = length_ref[0]
 
     def flash(zs, start, count):
-        rows = pl.ds(start, count)
-        token = ctx * TOK + (lax.broadcasted_iota(jnp.int32, (count, 1), 0) & (TOK - 1))
-        scores = []
-        for zp in zs:
-            code = jnp.where(
-                cached,
-                jnp.where(cache_base + zp * 32 < length, -1, FAR),
-                token_base + zp * 128,
-            )
-            product = lax.dot_general(
-                queries[rows], keys[zp], (((1,), (1,)), ((), ())), preferred_element_type=jnp.float32
-            )
-            scores.append(jnp.where(code <= token, product * SCALE2, MASKED))
-        before = maxima[rows, :1]
-        raised = before
-        for part_scores in scores:
-            raised = jnp.maximum(raised, jnp.max(part_scores, axis=1, keepdims=True))
-        factor = jnp.exp2(before - raised)
-        maxima[rows] = jnp.broadcast_to(raised, (count, 128))
-        total = totals[rows] * factor
-        value = acc[rows] * factor
-        for zp, part_scores in zip(zs, scores):
-            weights = jnp.exp2(part_scores - raised)
-            total = total + jnp.sum(weights, axis=1, keepdims=True)
-            value = value + jnp.dot(
-                weights.astype(jnp.bfloat16), keys[zp, :, :LATENT], preferred_element_type=jnp.float32
-            )
-        totals[rows] = total
-        acc[rows] = value
+        halves = []
+        for first_row in range(start, start + count, 256):
+            rows = pl.ds(first_row, 256)
+            token = ctx * TOK + (lax.broadcasted_iota(jnp.int32, (256, 1), 0) & (TOK - 1))
+            scores = []
+            for zp in zs:
+                code = jnp.where(
+                    cached,
+                    jnp.where(cache_base + zp * 32 < length, -1, FAR),
+                    token_base + zp * 128,
+                )
+                product = lax.dot_general(
+                    queries[rows], keys[zp], (((1,), (1,)), ((), ())), preferred_element_type=jnp.float32
+                )
+                scores.append(jnp.where(code <= token, product * SCALE2, MASKED))
+            halves.append((rows, scores))
+        for rows, scores in halves:
+            before = maxima[rows, :1]
+            raised = before
+            for part_scores in scores:
+                raised = jnp.maximum(raised, jnp.max(part_scores, axis=1, keepdims=True))
+            factor = jnp.exp2(before - raised)
+            maxima[rows] = jnp.broadcast_to(raised, (256, 128))
+            total = totals[rows] * factor
+            value = acc[rows] * factor
+            for zp, part_scores in zip(zs, scores):
+                weights = jnp.exp2(part_scores - raised)
+                total = total + jnp.sum(weights, axis=1, keepdims=True)
+                value = value + jnp.dot(
+                    weights.astype(jnp.bfloat16), keys[zp, :, :LATENT], preferred_element_type=jnp.float32
+                )
+            totals[rows] = total
+            acc[rows] = value
 
     for n in range(2):
 

time: 83.8 us -> 83.9 us (level)
  no operation moved by 1% of the time
where the time goes in v5:
time: 83.9 us; the launch traced here: 83.7 us
  Pallas kernels  81.3 us (97%)
  other arithmetic  1.01 us (1%)
    pallas_call x1, Pallas kernels, on_device(): pl.pallas_call(kernel, out_shape=jax.ShapeDtypeStruct((2, 512, 128), jnp....  81.3 us

profile of v5, /device:TPU:127, one launch (start us, length us, event | category | flops | bytes accessed | tf_op | source)
XLA Modules:
  0.0 83.7 jit_solution(16147146874010504252)
XLA Ops:
  0.7 81.3 %mla_prefill.1 = bf16[2,512,128]{2,1,0:T(8,128)(2,1)} custom-call(bf16[64,1536]{1,0:T(8,128)(2,1)} %query_hbm.1, bf16[64,576]{1,0:T(8,128)(2,1)} %span_hbm.1, bf16[16,576]{1,0:T(8,128)(2,1)} %cache_hbm.1, s32[1]{0:T(128)S(6)} %copy.8.length_ref, bf16[512,2048]{1,0:T(8,128)(2,1)} %kv_hbm.1, bf16[112,1024]{1,0:T(8,128)(2,1)} %bitcast.5), custom_call_target="tpu_custom_call" | custom-call | flops 8000000000 | bytes 4000000 | tf_op jit(solution)/shard_map/mla_prefill/pallas_call | solution.py:628
  81.9 1.0 %fusion = bf16[512,128]{1,0:T(8,128)(2,1)S(1)} fusion(bf16[2,512,128]{2,1,0:T(8,128)(2,1)} %mla_prefill.1), kind=kLoop, calls=%fused_computation.1 | loop fusion | flops 262144 | bytes 393216 | tf_op jit(solution)/shard_map/add | solution.py:677
  83.0 0.8 copy.7
